TPU v7x, 256 devices: a whole 4x4x8 slice. The times are simulated.
256 devices in a mesh: dp: 16 (over z, y_hi), expert: 16 (over y_lo, x, core).
Axes of the slice: x: 4, y: 4 (y_hi: 2, y_lo: 2; y = y_hi * 2 + y_lo), z: 8, core: 2. Of those that a mesh axis runs over, the one named last changes fastest.
Arguments:
- tokens: bfloat16 [2048, 7168], P('dp', 'expert'), may hold values from -6 to 6
- cotangent: bfloat16 [2048, 7168], P('dp', 'expert'), may hold values from -6 to 6
- gates: bfloat16 [2048, 2], P('dp'), may hold values from 0.19921875 to 2.5
- expert_ids: int32 [2048, 2], P('dp'), may hold values from 0 to 16, as said below
- w_gate: bfloat16 [16, 7168, 2048], P('dp', None, 'expert'), may hold values from -0.0625 to 0.0625
- w_up: bfloat16 [16, 7168, 2048], P('dp', None, 'expert'), may hold values from -0.0625 to 0.0625
- w_down: bfloat16 [16, 2048, 7168], P('dp', 'expert'), may hold values from -0.125 to 0.125
Outputs:
- grad_tokens: bfloat16 [2048, 7168], P('dp', 'expert')
- gate_grads: float32 [2048, 2], P('dp')
- grad_gate: bfloat16 [16, 7168, 2048], P('dp', None, 'expert')
- grad_up: bfloat16 [16, 7168, 2048], P('dp', None, 'expert')
- grad_down: bfloat16 [16, 2048, 7168], P('dp', 'expert')
Inputs may be any that keep to these rules, and one draw needn't show every extreme that they name: `expert_ids`: column 0 names one of the experts 0 to half of 16 minus 1 and column 1 one of the others, or the value 16 for a choice outside this window. The 128 tokens of one index of dp route at most 8 tokens to one expert; in each column one expert, the same for every index of dp, receives exactly 8 tokens from every index of dp.
All inputs are finite; a program needn't handle non-finite values.
Results may differ from a plain program's by a relative error of at most 0.024.
Values may be sent and summed in bfloat16 or wider, within the bound.
A program may use at most 128 MiB of HBM per device.

v0:
```python
import jax
import jax.numpy as jnp
from jax import lax
from jax.sharding import PartitionSpec as P

CAP = 8


def per_device(tokens, cotangent, gates, expert_ids, w_gate, w_up, w_down):
    experts = lax.axis_size("dp")
    labels = jnp.arange(experts, dtype=jnp.int32)
    first = expert_ids[:, 0:1] == labels[None, :]
    second = expert_ids[:, 1:2] == labels[None, :]
    member = jnp.logical_or(first, second)
    gate_f = gates.astype(jnp.float32)
    route = jnp.where(first, gate_f[:, 0:1], 0.0) + jnp.where(second, gate_f[:, 1:2], 0.0)
    places = jnp.cumsum(member.astype(jnp.int32), axis=0) - 1
    slot_ids = jnp.arange(CAP, dtype=jnp.int32)
    picker = jnp.logical_and(member.T[:, None, :], places.T[:, None, :] == slot_ids[None, :, None])
    picker_low = picker.astype(jnp.bfloat16)
    slot_gates = jnp.sum(jnp.where(picker, route.T[:, None, :], 0.0), axis=2).astype(jnp.bfloat16)
    slot_x = jnp.einsum(
        "est,tf->esf", picker_low, tokens, preferred_element_type=jnp.float32
    ).astype(jnp.bfloat16)
    slot_d = jnp.einsum(
        "est,tf->esf", picker_low, cotangent, preferred_element_type=jnp.float32
    ).astype(jnp.bfloat16)
    slot_x, slot_d, slot_g = (
        lax.all_to_all(slot_x, "dp", split_axis=0, concat_axis=0, tiled=True),
        lax.all_to_all(slot_d, "dp", split_axis=0, concat_axis=0, tiled=True),
        lax.all_to_all(slot_gates, "dp", split_axis=0, concat_axis=0, tiled=True),
    )
    slot_x, slot_d = (
        lax.all_gather(slot_x, "expert", axis=2, tiled=True),
        lax.all_gather(slot_d, "expert", axis=2, tiled=True),
    )
    total_rows = experts * CAP
    x_all = slot_x.reshape(total_rows, slot_x.shape[2])
    d_all = slot_d.reshape(total_rows, slot_d.shape[2])
    g_all = slot_g.reshape(total_rows).astype(jnp.float32)[:, None]
    gate_m = w_gate[0]
    up_m = w_up[0]
    down_m = w_down[0]
    pre_gate = jnp.dot(x_all, gate_m, preferred_element_type=jnp.float32)
    pre_up = jnp.dot(x_all, up_m, preferred_element_type=jnp.float32)
    sig = jax.nn.sigmoid(pre_gate)
    act = pre_gate * sig
    hidden = (act * pre_up).astype(jnp.bfloat16)
    back = lax.dot_general(
        d_all, down_m, (((1,), (1,)), ((), ())), preferred_element_type=jnp.float32
    )
    gate_part = jnp.sum(back * hidden.astype(jnp.float32), axis=1)
    dhid = g_all * back
    scaled = (g_all * d_all.astype(jnp.float32)).astype(jnp.bfloat16)
    grad_down = lax.dot_general(
        hidden, scaled, (((0,), (0,)), ((), ())), preferred_element_type=jnp.float32
    ).astype(jnp.bfloat16)
    d_gate = (dhid * pre_up * sig * (1.0 + pre_gate * (1.0 - sig))).astype(jnp.bfloat16)
    d_up = (dhid * act).astype(jnp.bfloat16)
    grad_gate = lax.dot_general(
        x_all, d_gate, (((0,), (0,)), ((), ())), preferred_element_type=jnp.float32
    ).astype(jnp.bfloat16)
    grad_up = lax.dot_general(
        x_all, d_up, (((0,), (0,)), ((), ())), preferred_element_type=jnp.float32
    ).astype(jnp.bfloat16)
    term = lax.dot_general(
        gate_m, d_gate, (((1,), (1,)), ((), ())), preferred_element_type=jnp.float32
    )
    feat_sums = lax.psum_scatter(
        (
            term
            + lax.dot_general(
                up_m, d_up, (((1,), (1,)), ((), ())), preferred_element_type=jnp.float32
            )
        ).astype(jnp.bfloat16),
        "expert",
        scatter_dimension=0,
        tiled=True,
    ).astype(jnp.float32)
    feat_sums = feat_sums.reshape(feat_sums.shape[0], experts, CAP)
    gate_back = lax.psum(gate_part, "expert").reshape(1, experts, CAP)
    feat_back, gate_back = (
        lax.all_to_all(
            feat_sums.astype(jnp.bfloat16), "dp", split_axis=1, concat_axis=1, tiled=True
        ).astype(feat_sums.dtype),
        lax.all_to_all(
            gate_back.astype(jnp.bfloat16), "dp", split_axis=1, concat_axis=1, tiled=True
        ).astype(gate_back.dtype),
    )
    slot_rows = feat_back.reshape(feat_back.shape[0], total_rows).T
    gate_flat = gate_back.reshape(total_rows)
    inside = expert_ids < experts
    safe_ids = jnp.where(inside, expert_ids, 0)
    slot_place = jnp.take_along_axis(places, safe_ids, axis=1)
    slot_index = safe_ids * CAP + jnp.maximum(slot_place, 0)
    first_rows = jnp.where(inside[:, 0:1], slot_rows[slot_index[:, 0]], 0.0)
    second_rows = jnp.where(inside[:, 1:2], slot_rows[slot_index[:, 1]], 0.0)
    grad_tokens = (first_rows + second_rows).astype(jnp.bfloat16)
    gate_grads = jnp.where(inside, gate_flat[slot_index], 0.0)
    return (grad_tokens, gate_grads, grad_gate[None], grad_up[None], grad_down[None])


def solution(mesh):
    in_specs = (
        P("dp", "expert"),
        P("dp", "expert"),
        P("dp", None),
        P("dp", None),
        P("dp", None, "expert"),
        P("dp", None, "expert"),
        P("dp", "expert", None),
    )
    out_specs = (
        P("dp", "expert"),
        P("dp", None),
        P("dp", None, "expert"),
        P("dp", None, "expert"),
        P("dp", "expert", None),
    )
    return jax.shard_map(
        per_device, mesh=mesh, in_specs=in_specs, out_specs=out_specs, check_vma=False
    )
```

profile of v0, /device:TPU:1, one launch (start us, length us, event | category | flops | bytes accessed | tf_op | source)
XLA Modules:
  0.0 318.0 jit_solution(10733379119206180612)
XLA Ops:
  7.2 0.8 slice_bitcast_fusion.3
  8.4 1.1 convolution_convert_fusion.3
  9.5 21.5 %all_to_all.26 = bf16[16,8,448]{2,1,0:T(8,128)(2,1)S(1)} all-to-all(bf16[16,8,448]{2,1,0:T(8,128)(2,1)S(1)} %convolution_convert_fusion.3), channel_id=1, replica_groups=mesh['dp'=16,'expert'=16] {'dp'}, dimensions={0} | all-to-all | bytes 229376 | tf_op jit(solution)/shard_map/all_to_all | solution.py:29
  31.1 1.4 copy.55
  32.8 12.6 %all_to_all.27 = bf16[16,8,448]{2,1,0:T(8,128)(2,1)S(1)} all-to-all(bf16[16,8,448]{2,1,0:T(8,128)(2,1)S(1)} %convolution_convert_fusion.4), channel_id=1, replica_groups=mesh['dp'=16,'expert'=16] {'dp'}, dimensions={0} | all-to-all | bytes 229376 | tf_op jit(solution)/shard_map/all_to_all | solution.py:30
  45.5 1.4 copy.53
  47.3 11.4 %all_to_all.28 = bf16[16,1,8]{2,1,0:T(2,128)(2,1)S(1)} all-to-all(bf16[16,1,8]{2,1,0:T(2,128)(2,1)S(1)} %copy.52), channel_id=1, replica_groups=mesh['dp'=16,'expert'=16] {'dp'}, dimensions={0} | all-to-all | bytes 512 | tf_op jit(solution)/shard_map/all_to_all | solution.py:31
  58.8 54.8 %all-gather.5.cloned.1.call-done = bf16[16,8,7168]{0,1,2:T(8,128)(2,1)} async-done(((bf16[16,8,448]{0,1,2:T(8,128)(2,1)}), bf16[16,8,7168]{0,1,2:T(8,128)(2,1)}) %all-gather.5.cloned.1.call-update) | async-done | bytes 1835024 | tf_op jit(solution)/shard_map/all_gather | solution.py:34
  113.6 15.2 %copy.56 = bf16[16,8,7168]{2,1,0:T(8,128)(2,1)} copy(bf16[16,8,7168]{0,1,2:T(8,128)(2,1)} %all-gather.5.cloned.1.call-done) | data formatting | bytes 3670016 | tf_op jit(solution)/shard_map/all_gather | solution.py:34
  128.8 2.5 fusion.7
  131.4 0.8 fusion.10
  132.2 68.3 %all-gather.3.cloned.1.call-done = bf16[16,8,7168]{0,1,2:T(8,128)(2,1)} async-done(((bf16[16,8,448]{0,1,2:T(8,128)(2,1)}), bf16[16,8,7168]{0,1,2:T(8,128)(2,1)}) %all-gather.3.cloned.1.call-update) | async-done | bytes 1835024 | tf_op jit(solution)/shard_map/all_gather | solution.py:35
  200.5 15.2 %copy.54 = bf16[16,8,7168]{2,1,0:T(8,128)(2,1)} copy(bf16[16,8,7168]{0,1,2:T(8,128)(2,1)} %all-gather.3.cloned.1.call-done) | data formatting | bytes 3670016 | tf_op jit(solution)/shard_map/all_gather | solution.py:35
  215.7 2.7 multiply_reduce_fusion
  219.1 0.8 copy-done.5
  219.9 1.9 fusion.4
  221.8 3.9 %copy.61 = bf16[7168,128]{1,0:T(8,128)(2,1)} copy(bf16[7168,128]{0,1:T(8,128)(2,1)} %fusion.4) | data formatting | bytes 3670016
  226.7 1.9 gather_fusion.3
  229.3 26.8 %psum.7 = bf16[128]{0:T(256)(128)(2,1)S(1)} all-reduce(f32[128]{0:T(128)S(1)} %get-tuple-element.41), channel_id=1, replica_groups=mesh['dp'=16,'expert'=16] {'expert'}, use_global_device_ids=true, to_apply=%region_4.5 | all-reduce | flops 128 | bytes 768 | tf_op jit(solution)/shard_map/psum | solution.py:81
  256.8 9.2 %all-to-all-start.4 = ((bf16[1,16,8]{2,0,1:T(2,128)(2,1)}), bf16[1,16,8]{2,0,1:T(2,128)(2,1)S(1)}, u32[]{:S(2)}, u32[]{:S(2)}) async-start(bf16[1,16,8]{2,0,1:T(2,128)(2,1)} %convert_element_type.117), calls=%async_computation.4 | async-start | bytes 16384 | tf_op jit(solution)/shard_map/all_to_all | solution.py:86
  266.0 3.6 %fusion.1 = bf16[1,7168,128]{2,1,0:T(8,128)(2,1)} fusion(bf16[128,128]{0,1:T(8,128)(2,1)S(1)} %get-tuple-element.45, bf16[16,8,7168]{2,1,0:T(8,128)(2,1)} %copy.56), kind=kOutput, calls=%fused_computation.9 | convolution fusion | flops 235798528 | bytes 3702784 | tf_op jit(solution)/shard_map/dot_general | solution.py:60
  269.6 1.9 fusion.3
  271.5 1.9 fusion.2
  273.4 1.3 all-to-all-done.4
  274.9 1.9 gather_fusion.2
  276.9 11.5 %reduce-scatter.4.cloned.1.call-done = bf16[448,128]{1,0:T(8,128)(2,1)} async-done(((bf16[7168,128]{1,0:T(8,128)(2,1)}), bf16[448,128]{1,0:T(8,128)(2,1)}) %reduce-scatter.4.cloned.1.call-update) | async-done | bytes 114704
  288.4 1.6 copy.62
  290.1 9.0 %all-to-all-start.3 = ((bf16[448,16,8]{0,2,1:T(8,128)(2,1)}), bf16[448,16,8]{0,2,1:T(8,128)(2,1)S(1)}, u32[]{:S(2)}, u32[]{:S(2)}) async-start(bf16[448,16,8]{0,2,1:T(8,128)(2,1)} %bitcast.14), calls=%async_computation.3 | async-start | bytes 262144 | tf_op jit(solution)/shard_map/all_to_all | solution.py:83
  299.7 9.3 %all-to-all-done.3 = bf16[448,16,8]{0,2,1:T(8,128)(2,1)S(1)} async-done(((bf16[448,16,8]{0,2,1:T(8,128)(2,1)}), bf16[448,16,8]{0,2,1:T(8,128)(2,1)S(1)}, u32[]{:S(2)}, u32[]{:S(2)}) %all-to-all-start.3) | async-done | bytes 114720 | tf_op jit(solution)/shard_map/all_to_all | solution.py:83
  309.1 0.8 gather_fusion.1
  309.8 0.8 gather_fusion
  310.7 0.8 copy.59
  (56 shorter events, 5.3 us)
Async XLA Ops:
  7.2 121.6 %copy-start = (bf16[1,7168,128]{2,1,0:T(8,128)(2,1)S(1)}, bf16[1,7168,128]{2,1,0:T(8,128)(2,1)}, u32[]{:S(2)}) copy-start(bf16[1,7168,128]{2,1,0:T(8,128)(2,1)} %param.11) | copy-start | bytes 5505028
  7.2 25.4 %copy-start.6 = (bf16[128,448]{0,1:T(8,128)(2,1)S(1)}, bf16[128,448]{0,1:T(8,128)(2,1)}, u32[]{:S(2)}) copy-start(bf16[128,448]{0,1:T(8,128)(2,1)} %param.8) | copy-start | bytes 344068
  7.2 106.4 %all-gather.5.cloned.1.call-start = ((), (), s32[]{:S(2)}) async-start(), calls=%async_computation.7 | async-start | bytes 15597568 | tf_op jit(solution)/shard_map/all_gather | solution.py:34
  32.5 14.5 %copy-start.8 = (bf16[128,2]{0,1:T(2,128)(2,1)S(1)}, bf16[128,2]{0,1:T(2,128)(2,1)}, u32[]{:S(2)}) copy-start(bf16[128,2]{0,1:T(2,128)(2,1)} %param.9) | copy-start | bytes 1540
  32.5 167.9 %all-gather.3.cloned.1.call-start = ((), (), s32[]{:S(2)}) async-start(), calls=%async_computation.6 | async-start | bytes 15597568 | tf_op jit(solution)/shard_map/all_gather | solution.py:35
  46.9 241.5 %reduce-scatter.4.cloned.1.call-start = ((), (), s32[]{:S(2)}) async-start(), calls=%async_computation.8 | async-start | bytes 1949696
  128.8 2.5 copy-start.1
  128.8 2.6 copy-start.4
  218.4 1.5 copy-start.5
  225.7 0.7 copy-start.7
  256.8 18.0 %all-to-all-start.4 = ((bf16[1,16,8]{2,0,1:T(2,128)(2,1)}), bf16[1,16,8]{2,0,1:T(2,128)(2,1)S(1)}, u32[]{:S(2)}, u32[]{:S(2)}) async-start(bf16[1,16,8]{2,0,1:T(2,128)(2,1)} %convert_element_type.117), calls=%async_computation.4 | async-start | bytes 16384 | tf_op jit(solution)/shard_map/all_to_all | solution.py:86
  266.0 3.6 %copy-start.3 = (bf16[16,8,7168]{2,1,0:T(8,128)(2,1)S(1)}, bf16[16,8,7168]{2,1,0:T(8,128)(2,1)}, u32[]{:S(2)}) copy-start(bf16[16,8,7168]{2,1,0:T(8,128)(2,1)} %copy.54) | copy-start | bytes 5505028
  269.6 1.9 copy-start.2
  290.1 19.0 %all-to-all-start.3 = ((bf16[448,16,8]{0,2,1:T(8,128)(2,1)}), bf16[448,16,8]{0,2,1:T(8,128)(2,1)S(1)}, u32[]{:S(2)}, u32[]{:S(2)}) async-start(bf16[448,16,8]{0,2,1:T(8,128)(2,1)} %bitcast.14), calls=%async_computation.3 | async-start | bytes 262144 | tf_op jit(solution)/shard_map/all_to_all | solution.py:83
Sparse Core Ops, SparseCore 0:
  32.7 80.8 all-gather.4
  116.0 84.4 all-gather.2
  225.8 62.5 reduce-scatter.3
where the time goes:
time: 322 us; the launch traced here: 318 us
  waiting for transfers between devices  145 us (45%)
  blocking collectives  72.3 us (22%)
  local copies, waits for them, and re-layouts  49.9 us (15%)
  starting transfers between devices  18.3 us (6%)
  matrix products  17.3 us (5%)
  between operations  14 us (4%)
    all_gather x1, waiting for transfers between devices, per_device(): lax.all_gather(slot_d, 'expert', axis=2, tiled=True)  68.3 us
    all_gather x1, waiting for transfers between devices, per_device(): lax.all_gather(slot_x, 'expert', axis=2, tiled=True)  54.8 us
    psum x1, blocking collectives, per_device(): gate_back = lax.psum(gate_part, 'expert').reshape(1, experts, CAP)  26.8 us
    all_to_all x1, blocking collectives, per_device(): lax.all_to_all(slot_x, 'dp', split_axis=0, concat_axis=0, tiled=True)  21.5 us
    all_gather x1, local copies, waits for them, and re-layouts, per_device(): lax.all_gather(slot_x, 'expert', axis=2, tiled=True)  15.2 us
    all_gather x1, local copies, waits for them, and re-layouts, per_device(): lax.all_gather(slot_d, 'expert', axis=2, tiled=True)  15.2 us
    all_to_all x1, blocking collectives, per_device(): lax.all_to_all(slot_d, 'dp', split_axis=0, concat_axis=0, tiled=True)  12.6 us
    unnamed x4, waiting for transfers between devices  11.6 us
  transfers between devices with their start and end apart: 5, of which 5 were waited for; matrix products, arithmetic and copies ran while one was open for 11% of the time, Pallas kernels for 0%

commit v1 on v0

v1 whole, which is shorter than its diff:
```python
import functools

import jax
import jax.numpy as jnp
from jax import lax
from jax.experimental import pallas as pl
from jax.experimental.pallas import tpu as pltpu
from jax.sharding import PartitionSpec as P

MESH = pl.DeviceIdType.MESH
BF = jnp.bfloat16
F32 = jnp.float32

CAP = 8
NDP = 16
NEX = 16
F = 448
FA = 256
FB = F - FA
HB = FB // 2
HA = FA // 2
C = 2 * F
D = NEX * F
HID = 128
TOK = 128
SLOTS = NDP * CAP
RB = F + 16


def iota(shape, dim):
    return lax.broadcasted_iota(jnp.int32, shape, dim)


def split_gate(row):
    hi = row.astype(BF).astype(F32)
    lo = row - hi
    r = iota((16, row.shape[1]), 0)
    return jnp.where(r == 0, hi, jnp.where(r == 1, lo, 0.0)).astype(BF)


def comm_kernel(
    tok_ref, cot_ref, ids_ref, gates_ref, wg_hbm, wu_hbm, wd_hbm,
    ret_out, pick_out, all_out, dd_out, hg_out,
    wgu, wd, ext, sa, sb, ra, rb, al, pre, back, dd, hg, tsend, tsib, rsend, rrecv, rpad, retb, ret,
    w_sem, out_sem, da_send, da_recv, db_send, db_recv, g_send, g_recv, sib_send, sib_recv,
    ts_send, ts_recv, r_send, r_recv, b_send, b_recv,
):
    me = lax.axis_index("dp")
    j = lax.axis_index("expert")
    y, x, c = j // 8, (j // 2) % 4, j % 2

    def dev(yy, xx, cc):
        return yy * 8 + xx * 2 + cc

    xr, xl, xo = (x + 1) % 4, (x + 3) % 4, (x + 2) % 4
    yo = 1 - y
    sib, xp, xm, yp = dev(y, x, 1 - c), dev(y, xr, c), dev(y, xl, c), dev(yo, x, c)

    barrier = pltpu.get_barrier_semaphore()
    for i in range(1, NDP):
        pl.semaphore_signal(barrier, inc=1, device_id=((me + i) % NDP, j), device_id_type=MESH)
    others = [(sib,)]
    chips = [(yy, xx) for yy in (y, yo) for xx in (x, xr, xl, xo)][1:]
    for yy, xx in chips:
        pl.semaphore_signal(barrier, inc=1, device_id=(me, dev(yy, xx, c)), device_id_type=MESH)
    pl.semaphore_signal(barrier, inc=1, device_id=(me, sib), device_id_type=MESH)

    loads = [
        pltpu.make_async_copy(wg_hbm.at[0], wgu.at[:, 0:HID], w_sem.at[0]),
        pltpu.make_async_copy(wu_hbm.at[0], wgu.at[:, HID : 2 * HID], w_sem.at[1]),
        pltpu.make_async_copy(wd_hbm.at[0], wd, w_sem.at[2]),
    ]
    for load in loads:
        load.start()

    col = iota((TOK, 256), 1)
    ids = ids_ref[...]
    chosen = jnp.where(col < 128, ids[:, 0:1], ids[:, 1:2])
    member = chosen == col // 16
    tri = (iota((TOK, TOK), 1) < iota((TOK, TOK), 0)).astype(F32).astype(BF)
    before = jnp.dot(tri, member.astype(F32).astype(BF), preferred_element_type=F32)
    pick = jnp.where(
        jnp.logical_and(member, before == (col % 8).astype(F32)), 1.0, 0.0
    )
    is_x = (col % 16) < 8
    pick_out[...] = pick.astype(BF)
    pick2 = jnp.concatenate(
        [jnp.where(is_x, pick, 0.0), jnp.where(is_x, 0.0, pick)], axis=0
    ).astype(BF)
    ext[:, 384:512] = jnp.zeros((2 * TOK, 128), BF)
    ext[0:TOK, 0:F] = tok_ref[...]
    ext[TOK : 2 * TOK, 0:F] = cot_ref[...]
    gates = gates_ref[...].astype(F32)
    lane = iota((TOK, 128), 1)
    ext[0:TOK, 384:512] = jnp.where(
        lane == 64,
        gates[:, 0:1],
        jnp.where(lane == 65, gates[:, 1:2], ext[0:TOK, 384:512].astype(F32)),
    ).astype(BF)
    slots = lax.dot_general(
        pick2, ext[...], (((0,), (0,)), ((), ())), preferred_element_type=F32
    ).astype(BF)
    sa[...] = slots[:, 0:256].reshape(NDP, 16, 256)
    sb[...] = slots[:, 256:512].reshape(NDP, 16, 256)

    pl.semaphore_wait(barrier, NDP - 1 + len(chips) + 1)

    def dispatch(src, dst, send, recv):
        copies = []
        for i in range(1, NDP):
            to = (me + i) % NDP
            copy = pltpu.make_async_remote_copy(
                src_ref=src.at[to], dst_ref=dst.at[me],
                send_sem=send.at[i], recv_sem=recv.at[i],
                device_id=(to, j), device_id_type=MESH,
            )
            copy.start()
            copies.append(copy)
        dst[pl.ds(me, 1)] = src[pl.ds(me, 1)]
        return copies

    copies_a = dispatch(sa, ra, da_send, da_recv)
    copies_b = dispatch(sb, rb, db_send, db_recv)

    r = iota((256, 256), 0)
    k = iota((256, 256), 1)
    kk = k % 128
    perm = jnp.where(r == (kk // 8) * 16 + (k // 128) * 8 + kk % 8, 1.0, 0.0).astype(BF)

    def turned(buf):
        return lax.dot_general(
            buf[...].reshape(256, 256), perm, (((0,), (0,)), ((), ())),
            preferred_element_type=F32,
        )

    def rows(b, lo, n):
        return al.at[pl.ds(pl.multiple_of(b * F + lo, 16), n)]

    sends = []

    def push(b, lo, n, to, s):
        copy = pltpu.make_async_remote_copy(
            src_ref=rows(b, lo, n), dst_ref=rows(b, lo, n),
            send_sem=g_send.at[s], recv_sem=g_recv.at[s],
            device_id=(me, to), device_id_type=MESH,
        )
        copy.start()
        sends.append(copy)

    def share(b, lo, n, s):
        copy = pltpu.make_async_remote_copy(
            src_ref=rows(b, lo, n), dst_ref=rows(b, lo, n),
            send_sem=sib_send.at[s], recv_sem=sib_recv.at[s],
            device_id=(me, sib), device_id_type=MESH,
        )
        copy.start()
        sends.append(copy)

    def got(b, lo, n, s):
        pltpu.make_async_remote_copy(
            src_ref=rows(b, lo, n), dst_ref=rows(b, lo, n),
            send_sem=g_send.at[s], recv_sem=g_recv.at[s],
            device_id=(me, sib), device_id_type=MESH,
        ).wait_recv()

    def shared(b, lo, n, s):
        pltpu.make_async_remote_copy(
            src_ref=rows(b, lo, n), dst_ref=rows(b, lo, n),
            send_sem=sib_send.at[s], recv_sem=sib_recv.at[s],
            device_id=(me, sib), device_id_type=MESH,
        ).wait_recv()

    b_own, b_xr, b_xl, b_xo = (dev(y, xx, c) for xx in (x, xr, xl, xo))
    o_own, o_xr, o_xl, o_xo = (dev(yo, xx, c) for xx in (x, xr, xl, xo))

    for copy in copies_a:
        copy.wait_recv()
    al[pl.ds(pl.multiple_of(j * F, 16), FA), :] = turned(ra).astype(BF)
    push(b_own, 0, FA, yp, 0)
    push(b_own, 0, FA, xp, 1)
    push(b_own, 0, FA, xm, 2)
    share(b_own, 0, FA, 0)

    for copy in copies_b:
        copy.wait_recv()
    second = turned(rb)
    al[pl.ds(pl.multiple_of(j * F + FA, 16), FB), :] = second[0:FB].astype(BF)
    gate_row = jnp.where(me < NDP // 2, second[FB : FB + 1, 0:128], second[FB + 1 : FB + 2, 0:128])
    push(b_own, FA, FB, yp, 3)
    push(b_own, FA, FB, xp, 4)
    push(b_own, FA, FB, xm, 5)
    share(b_own, FA, FB, 1)

    pre[...] = jnp.zeros_like(pre)
    back[...] = jnp.zeros_like(back)
    for load in loads:
        load.wait()

    def forward(chip):
        at = pl.ds(pl.multiple_of(chip * C, 128), C)
        block = al[at, :]
        pre[...] += lax.dot_general(
            block[:, 0:128], wgu[at, :], (((0,), (0,)), ((), ())), preferred_element_type=F32
        )
        back[...] += jnp.dot(wd[:, at], block[:, 128:256], preferred_element_type=F32)

    got(o_own, 0, FA, 0)
    push(o_own, 0, FA, xp, 6)
    push(o_own, 0, FA, xm, 7)
    share(o_own, 0, FA, 2)
    got(b_xl, FA, FB, 4)
    push(b_xl, FA, HB, xp, 8)
    push(b_xl, FA, FB, yp, 9)
    share(b_xl, FA, FB, 3)
    got(b_xr, FA, FB, 5)
    push(b_xr, FA + HB, HB, xm, 10)
    push(b_xr, FA, FB, yp, 11)
    share(b_xr, FA, FB, 4)
    got(b_xl, 0, FA, 1)
    push(b_xl, 0, HA, xp, 12)
    share(b_xl, 0, FA, 5)
    got(b_xr, 0, FA, 2)
    push(b_xr, HA, HA, xm, 13)
    share(b_xr, 0, FA, 6)

    sib_own = dev(y, x, 1 - c)
    shared(sib_own, 0, FA, 0)
    shared(sib_own, FA, FB, 1)
    forward(y * 4 + x)

    got(b_xo, FA, HB, 8)
    push(b_xo, FA, HB, yp, 14)
    share(b_xo, FA, HB, 7)
    got(b_xo, FA + HB, HB, 10)
    push(b_xo, FA + HB, HB, yp, 15)
    share(b_xo, FA + HB, HB, 8)
    got(o_xl, 0, FA, 6)
    push(o_xl, 0, HA, xp, 16)
    share(o_xl, 0, FA, 9)
    got(o_xr, 0, FA, 7)
    push(o_xr, HA, HA, xm, 17)
    share(o_xr, 0, FA, 10)
    got(o_own, FA, FB, 3)
    share(o_own, FA, FB, 11)

    n_xr, n_xl, n_xo = (dev(y, xx, 1 - c) for xx in (xr, xl, xo))
    m_own, m_xr, m_xl, m_xo = (dev(yo, xx, 1 - c) for xx in (x, xr, xl, xo))
    shared(n_xl, FA, FB, 3)
    shared(n_xl, 0, FA, 5)
    forward(y * 4 + xl)
    got(o_xl, FA, FB, 9)
    share(o_xl, FA, FB, 12)
    shared(n_xr, FA, FB, 4)
    shared(n_xr, 0, FA, 6)
    forward(y * 4 + xr)
    got(o_xr, FA, FB, 11)
    share(o_xr, FA, FB, 13)
    shared(m_own, 0, FA, 2)
    shared(m_own, FA, FB, 11)
    forward(yo * 4 + x)
    got(b_xo, 0, HA, 12)
    share(b_xo, 0, HA, 14)
    got(b_xo, HA, HA, 13)
    share(b_xo, HA, HA, 15)
    shared(m_xl, 0, FA, 9)
    shared(m_xl, FA, FB, 12)
    forward(yo * 4 + xl)
    shared(m_xr, 0, FA, 10)
    shared(m_xr, FA, FB, 13)
    forward(yo * 4 + xr)
    got(o_xo, 0, HA, 16)
    share(o_xo, 0, HA, 16)
    got(o_xo, HA, HA, 17)
    share(o_xo, HA, HA, 17)
    got(o_xo, FA, HB, 14)
    share(o_xo, FA, HB, 18)
    got(o_xo, FA + HB, HB, 15)
    share(o_xo, FA + HB, HB, 19)
    shared(n_xo, FA, HB, 7)
    shared(n_xo, FA + HB, HB, 8)
    shared(n_xo, 0, HA, 14)
    shared(n_xo, HA, HA, 15)
    forward(y * 4 + xo)
    shared(m_xo, 0, HA, 16)
    shared(m_xo, HA, HA, 17)
    shared(m_xo, FA, HB, 18)
    shared(m_xo, FA + HB, HB, 19)
    forward(yo * 4 + xo)

    keep = pltpu.make_async_copy(al, all_out, out_sem)
    keep.start()

    turned_pre = pre[...].T
    pg, pu = turned_pre[0:HID], turned_pre[HID : 2 * HID]
    sig = jax.nn.sigmoid(pg)
    act = pg * sig
    hidden = act * pu
    bk = back[...]
    gate_terms = split_gate(
        jnp.sum(bk * hidden.astype(BF).astype(F32), axis=0, keepdims=True)
    )
    dhid = gate_row * bk
    dd[0:HID, :] = (dhid * pu * sig * (1.0 + pg * (1.0 - sig))).astype(BF)
    dd[HID : 2 * HID, :] = (dhid * act).astype(BF)
    hg[...] = (hidden * gate_row).astype(BF)
    dd_out[...] = dd[...]
    hg_out[...] = hg[...]

    def term(b):
        at = pl.ds(pl.multiple_of(b * F, 16), F)
        return jnp.dot(wgu[at, :], dd[...], preferred_element_type=F32)

    order = [(yo, xo), (yo, xl), (yo, xr), (y, xo), (yo, x), (y, xl), (y, xr), (y, x)]
    ts_copies = []
    for n, (yy, xx) in enumerate(order):
        tsend[n, 0:F, :] = term(dev(yy, xx, 1 - c)).astype(BF)
        tsend[n, F:RB, :] = gate_terms
        copy = pltpu.make_async_remote_copy(
            src_ref=tsend.at[n], dst_ref=tsib.at[n],
            send_sem=ts_send.at[n], recv_sem=ts_recv.at[n],
            device_id=(me, sib), device_id_type=MESH,
        )
        copy.start()
        ts_copies.append(copy)

    def gate_total(*blocks):
        total = sum(block.astype(F32) for block in blocks)
        return jnp.sum(total, axis=0, keepdims=True)

    r_copies = []
    for n, (yy, xx) in enumerate(order):
        part = term(dev(yy, xx, c))
        ts_copies[n].wait_recv()
        part = part + tsib[n, 0:F, :].astype(F32)
        gate_part = gate_total(gate_terms, tsib[n, F:RB, :])
        if n < 7:
            rsend[n, 0:F, :] = part.astype(BF)
            rsend[n, F:RB, :] = split_gate(gate_part)
            copy = pltpu.make_async_remote_copy(
                src_ref=rsend.at[n], dst_ref=rrecv.at[n],
                send_sem=r_send.at[n], recv_sem=r_recv.at[n],
                device_id=(me, dev(yy, xx, c)), device_id_type=MESH,
            )
            copy.start()
            r_copies.append(copy)
        else:
            total, gate_sum = part, gate_part
    for n in range(6, -1, -1):
        r_copies[n].wait_recv()
        total = total + rrecv[n, 0:F, :].astype(F32)
        gate_sum = gate_sum + gate_total(rrecv[n, F:RB, :])

    rpad[0:F, :] = total.astype(BF)
    rpad[F:RB, :] = split_gate(gate_sum)
    rpad[RB:512, :] = jnp.zeros((512 - RB, SLOTS), BF)
    r = iota((256, SLOTS), 0)
    k = iota((256, SLOTS), 1)
    here = k == (r // 16) * 8 + r % 8
    low = (r % 16) < 8
    first = jnp.where(jnp.logical_and(here, low), 1.0, 0.0).astype(BF)
    other = jnp.where(jnp.logical_and(here, jnp.logical_not(low)), 1.0, 0.0).astype(BF)
    nt = (((1,), (1,)), ((), ()))
    back_rows = lax.dot_general(first, rpad[0:256, :], nt, preferred_element_type=F32)
    back_rows += lax.dot_general(other, rpad[256:512, :], nt, preferred_element_type=F32)
    retb[...] = back_rows.astype(BF).reshape(NDP, 16, 256)
    b_copies = dispatch(retb, ret, b_send, b_recv)
    for copy in b_copies:
        copy.wait_recv()
    ret_out[...] = ret[...].reshape(256, 256)

    for copy in copies_a + copies_b + sends + ts_copies + r_copies + b_copies:
        copy.wait_send()
    keep.wait()


def grad_kernel(al, dd, hg, ret, pick, gt_out, gg_out, gate_out, up_out, down_out):
    nt = (((1,), (1,)), ((), ()))
    block = al[...]
    both = lax.dot_general(block[:, 0:128], dd[...], nt, preferred_element_type=F32)
    gate_out[0] = both[:, 0:HID].astype(BF)
    up_out[0] = both[:, HID : 2 * HID].astype(BF)
    down_out[0] = lax.dot_general(
        hg[...], block[:, 128:256], nt, preferred_element_type=F32
    ).astype(BF)

    @pl.when(pl.program_id(0) == 0)
    def _():
        col = iota((TOK, 256), 1)
        is_x = (col % 16) < 8
        picks = pick[...].astype(F32)
        px = jnp.where(is_x, picks, 0.0).astype(BF)
        pd = jnp.where(is_x, 0.0, picks).astype(BF)
        rows = ret[...]
        gt_out[:, 0:FA] = jnp.dot(px, rows, preferred_element_type=F32).astype(BF)
        one = jnp.dot(pd[:, 0:128], rows[0:128], preferred_element_type=F32)
        two = jnp.dot(pd[:, 128:256], rows[128:256], preferred_element_type=F32)
        gt_out[:, FA:F] = (one + two)[:, 0:FB].astype(BF)
        gg_out[:, 0:1] = one[:, FB : FB + 1] + one[:, FB + 1 : FB + 2]
        gg_out[:, 1:2] = two[:, FB : FB + 1] + two[:, FB + 1 : FB + 2]


def per_device(tokens, cotangent, gates, expert_ids, w_gate, w_up, w_down):
    vmem = pl.BlockSpec(memory_space=pltpu.VMEM)
    anym = pl.BlockSpec(memory_space=pl.ANY)
    dma = pltpu.SemaphoreType.DMA
    ret, pick, al, dd, hg = pl.pallas_call(
        comm_kernel,
        out_shape=[
            jax.ShapeDtypeStruct((256, 256), BF),
            jax.ShapeDtypeStruct((TOK, 256), BF),
            jax.ShapeDtypeStruct((D, 256), BF),
            jax.ShapeDtypeStruct((2 * HID, SLOTS), BF),
            jax.ShapeDtypeStruct((HID, SLOTS), BF),
        ],
        in_specs=[vmem] * 4 + [anym] * 3,
        out_specs=[vmem, vmem, anym, vmem, vmem],
        scratch_shapes=[
            pltpu.VMEM((D, 2 * HID), BF),
            pltpu.VMEM((HID, D), BF),
            pltpu.VMEM((2 * TOK, 512), BF),
            pltpu.VMEM((NDP, 16, 256), BF),
            pltpu.VMEM((NDP, 16, 256), BF),
            pltpu.VMEM((NDP, 16, 256), BF),
            pltpu.VMEM((NDP, 16, 256), BF),
            pltpu.VMEM((D, 256), BF),
            pltpu.VMEM((SLOTS, 2 * HID), F32),
            pltpu.VMEM((HID, SLOTS), F32),
            pltpu.VMEM((2 * HID, SLOTS), BF),
            pltpu.VMEM((HID, SLOTS), BF),
            pltpu.VMEM((8, RB, SLOTS), BF),
            pltpu.VMEM((8, RB, SLOTS), BF),
            pltpu.VMEM((7, RB, SLOTS), BF),
            pltpu.VMEM((7, RB, SLOTS), BF),
            pltpu.VMEM((512, SLOTS), BF),
            pltpu.VMEM((NDP, 16, 256), BF),
            pltpu.VMEM((NDP, 16, 256), BF),
            dma((3,)), dma(()),
            dma((NDP,)), dma((NDP,)), dma((NDP,)), dma((NDP,)),
            dma((18,)), dma((18,)), dma((20,)), dma((20,)),
            dma((8,)), dma((8,)), dma((7,)), dma((7,)),
            dma((NDP,)), dma((NDP,)),
        ],
        compiler_params=pltpu.CompilerParams(
            collective_id=0, has_side_effects=True, vmem_limit_bytes=40 * 1024 * 1024
        ),
        name="comm",
    )(tokens, cotangent, expert_ids, gates, w_gate, w_up, w_down)

    step = 2 * C
    whole = lambda *shape: pl.BlockSpec(shape, lambda i: (0,) * len(shape))
    return pl.pallas_call(
        grad_kernel,
        grid=(D // step,),
        out_shape=[
            jax.ShapeDtypeStruct((TOK, F), BF),
            jax.ShapeDtypeStruct((TOK, 2), F32),
            jax.ShapeDtypeStruct((1, D, HID), BF),
            jax.ShapeDtypeStruct((1, D, HID), BF),
            jax.ShapeDtypeStruct((1, HID, D), BF),
        ],
        in_specs=[
            pl.BlockSpec((step, 256), lambda i: (i, 0)),
            whole(2 * HID, SLOTS),
            whole(HID, SLOTS),
            whole(256, 256),
            whole(TOK, 256),
        ],
        out_specs=[
            whole(TOK, F),
            whole(TOK, 2),
            pl.BlockSpec((1, step, HID), lambda i: (0, i, 0)),
            pl.BlockSpec((1, step, HID), lambda i: (0, i, 0)),
            pl.BlockSpec((1, HID, step), lambda i: (0, 0, i)),
        ],
        compiler_params=pltpu.CompilerParams(vmem_limit_bytes=32 * 1024 * 1024),
        name="grads",
    )(al, dd, hg, ret, pick)


def solution(mesh):
    in_specs = (
        P("dp", "expert"),
        P("dp", "expert"),
        P("dp", None),
        P("dp", None),
        P("dp", None, "expert"),
        P("dp", None, "expert"),
        P("dp", "expert", None),
    )
    out_specs = (
        P("dp", "expert"),
        P("dp", None),
        P("dp", None, "expert"),
        P("dp", None, "expert"),
        P("dp", "expert", None),
    )
    return jax.shard_map(
        per_device, mesh=mesh, in_specs=in_specs, out_specs=out_specs, check_vma=False
    )
```

time: 322 us -> 77.7 us (0.24); the launches traced: 318 us -> 77.5 us
  waiting for transfers between devices: 145 us -> 0 us
  blocking collectives: 72.3 us -> 0 us
  Pallas kernels: 0 us -> 67.4 us
  local copies, waits for them, and re-layouts: 49.9 us -> 9.46 us
  starting transfers between devices: 18.3 us -> 0 us
  matrix products: 17.3 us -> 0 us
  between operations: 14 us -> 0.67 us
    all_gather x2 -> x0, waiting for transfers between devices: 123 us -> none  [the longest x1 68.3 us: per_device(): lax.all_gather(slot_d, 'expert', axis=2, tiled=True)]
    pallas_call x0 -> x2, Pallas kernels: none -> 67.4 us  [the longest x1 63.3 us: per_device(): pl.pallas_call(comm_kernel, out_shape=[jax.ShapeDtypeStruct((256, 256), B...]
    all_to_all x3 -> x0, blocking collectives: 45.6 us -> none  [the longest x1 21.5 us: per_device(): lax.all_to_all(slot_x, 'dp', split_axis=0, concat_axis=0, tiled=True)]
    all_gather x2 -> x0, local copies, waits for them, and re-layouts: 30.4 us -> none  [the longest x1 15.2 us: per_device(): lax.all_gather(slot_x, 'expert', axis=2, tiled=True)]
    psum x1 -> x0, blocking collectives: 26.8 us -> none  [per_device(): gate_back = lax.psum(gate_part, 'expert').reshape(1, experts, CAP)]
    all_to_all x2 -> x0, starting transfers between devices: 18.2 us -> none  [the longest x1 9.16 us: per_device(): lax.all_to_all(gate_back.astype(jnp.bfloat16), 'dp', split_axis=1, concat...]
    dot_general x10 -> x0, matrix products: 17.3 us -> none  [the longest x1 3.56 us: per_device(): lax.dot_general(x_all, d_gate, (((0,), (0,)), ((), ())), preferred_elemen...]
    unnamed x4 -> x0, waiting for transfers between devices: 11.6 us -> none
  transfers between devices with their start and end apart: 5 -> 0, of which waited for: 5 -> 0; matrix products, arithmetic and copies ran while one was open for 11% -> 0% of each run, Pallas kernels for 0% -> 0%
where the time goes in v1:
time: 77.7 us; the launch traced here: 77.5 us
  Pallas kernels  67.4 us (87%)
  local copies, waits for them, and re-layouts  9.46 us (12%)
    pallas_call x1, Pallas kernels, per_device(): pl.pallas_call(comm_kernel, out_shape=[jax.ShapeDtypeStruct((256, 256), B...  63.3 us
    unnamed x10, local copies, waits for them, and re-layouts  8.06 us
    pallas_call x1, Pallas kernels, per_device(): pl.pallas_call(grad_kernel, grid=(D // step,), out_shape=[jax.ShapeDtypeS...  4.05 us

profile of v1, /device:TPU:1, one launch (start us, length us, event | category | flops | bytes accessed | tf_op | source)
XLA Modules:
  0.0 77.5 jit_solution(2784023598175597853)
XLA Ops:
  0.6 0.8 %copy.15.gates_ref = bf16[128,2]{1,0:T(8,128)(2,1)S(1)} copy(bf16[128,2]{0,1:T(2,128)(2,1)} %param.9) | data formatting | bytes 1024 | tf_op args[2]
  1.4 0.8 %copy.14.ids_ref = s32[128,2]{1,0:T(8,128)S(1)} copy(s32[128,2]{0,1:T(2,128)} %param.10) | data formatting | bytes 2048 | tf_op args[3]
  2.2 1.0 %copy.12.tok_ref = bf16[128,448]{1,0:T(8,128)(2,1)S(1)} copy(bf16[128,448]{0,1:T(8,128)(2,1)} %param.7) | data formatting | bytes 229376 | tf_op args[0]
  3.2 1.0 %copy.13.cot_ref = bf16[128,448]{1,0:T(8,128)(2,1)S(1)} copy(bf16[128,448]{0,1:T(8,128)(2,1)} %param.8) | data formatting | bytes 229376 | tf_op args[1]
  4.2 0.0 copy-start
  4.2 1.5 %copy-done = bf16[1,7168,128]{2,1,0:T(8,128)(2,1)S(1)} copy-done((bf16[1,7168,128]{2,1,0:T(8,128)(2,1)S(1)}, bf16[1,7168,128]{2,1,0:T(8,128)(2,1)}, u32[]{:S(2)}) %copy-start) | copy-done | bytes 1835032
  5.7 0.0 copy-start.1
  5.7 1.5 %copy-done.1 = bf16[1,7168,128]{2,1,0:T(8,128)(2,1)S(1)} copy-done((bf16[1,7168,128]{2,1,0:T(8,128)(2,1)S(1)}, bf16[1,7168,128]{2,1,0:T(8,128)(2,1)}, u32[]{:S(2)}) %copy-start.1) | copy-done | bytes 1835032
  7.2 0.0 copy-start.2
  7.2 1.5 %copy-done.2 = bf16[1,128,7168]{2,1,0:T(8,128)(2,1)S(1)} copy-done((bf16[1,128,7168]{2,1,0:T(8,128)(2,1)S(1)}, bf16[1,128,7168]{2,1,0:T(8,128)(2,1)}, u32[]{:S(2)}) %copy-start.2) | copy-done | bytes 1835032
  8.7 63.3 %comm.1 = (bf16[256,256]{1,0:T(8,128)(2,1)S(1)}, bf16[128,256]{1,0:T(8,128)(2,1)S(1)}, bf16[7168,256]{1,0:T(8,128)(2,1)S(1)}, bf16[256,128]{1,0:T(8,128)(2,1)S(1)}, bf16[128,128]{1,0:T(8,128)(2,1)S(1)}) custom-call(bf16[128,448]{1,0:T(8,128)(2,1)S(1)} %copy.12.tok_ref, bf16[128,448]{1,0:T(8,128)(2,1)S(1)} %copy.13.cot_ref, s32[128,2]{1,0:T(8,128)S(1)} %copy.14.ids_ref, ...), custom_call_target="tpu_custom_call" | custom-call | tf_op jit(solution)/shard_map/comm/pallas_call | solution.py:406
  72.0 4.1 %grads.1 = (bf16[128,448]{1,0:T(8,128)(2,1)S(1)}, f32[128,2]{1,0:T(8,128)S(1)}, bf16[1,7168,128]{2,1,0:T(8,128)(2,1)}, bf16[1,7168,128]{2,1,0:T(8,128)(2,1)}, bf16[1,128,7168]{2,1,0:T(8,128)(2,1)}) custom-call(bf16[7168,256]{1,0:T(8,128)(2,1)S(1)} %get-tuple-element.10.al, bf16[256,128]{1,0:T(8,128)(2,1)S(1)} %get-tuple-element.11.dd, ...), custom_call_target="tpu_custom_call" | custom-call | tf_op jit(solution)/shard_map/grads/pallas_call | solution.py:451
  76.1 0.8 copy.16
  76.9 0.6 copy.17
Async XLA Ops:
  4.2 1.5 %copy-start = (bf16[1,7168,128]{2,1,0:T(8,128)(2,1)S(1)}, bf16[1,7168,128]{2,1,0:T(8,128)(2,1)}, u32[]{:S(2)}) copy-start(bf16[1,7168,128]{2,1,0:T(8,128)(2,1)} %wg_hbm.1) | copy-start | bytes 5505028
  5.7 1.5 %copy-start.1 = (bf16[1,7168,128]{2,1,0:T(8,128)(2,1)S(1)}, bf16[1,7168,128]{2,1,0:T(8,128)(2,1)}, u32[]{:S(2)}) copy-start(bf16[1,7168,128]{2,1,0:T(8,128)(2,1)} %wu_hbm.1) | copy-start | bytes 5505028
  7.2 1.5 %copy-start.2 = (bf16[1,128,7168]{2,1,0:T(8,128)(2,1)S(1)}, bf16[1,128,7168]{2,1,0:T(8,128)(2,1)}, u32[]{:S(2)}) copy-start(bf16[1,128,7168]{2,1,0:T(8,128)(2,1)} %wd_hbm.1) | copy-start | bytes 5505028

commit v2 on v1

--- a/solution.py
+++ b/solution.py
@@ -39,7 +39,7 @@
 
 
 def comm_kernel(
-    tok_ref, cot_ref, ids_ref, gates_ref, wg_hbm, wu_hbm, wd_hbm,
+    tok_hbm, cot_hbm, ids_ref, gates_ref, wg_hbm, wu_hbm, wd_hbm,
     ret_out, pick_out, all_out, dd_out, hg_out,
     wgu, wd, ext, sa, sb, ra, rb, al, pre, back, dd, hg, tsend, tsib, rsend, rrecv, rpad, retb, ret,
     w_sem, out_sem, da_send, da_recv, db_send, db_recv, g_send, g_recv, sib_send, sib_recv,
@@ -56,10 +56,11 @@
     yo = 1 - y
     sib, xp, xm, yp = dev(y, x, 1 - c), dev(y, xr, c), dev(y, xl, c), dev(yo, x, c)
 
+    started = []
+
     barrier = pltpu.get_barrier_semaphore()
     for i in range(1, NDP):
         pl.semaphore_signal(barrier, inc=1, device_id=((me + i) % NDP, j), device_id_type=MESH)
-    others = [(sib,)]
     chips = [(yy, xx) for yy in (y, yo) for xx in (x, xr, xl, xo)][1:]
     for yy, xx in chips:
         pl.semaphore_signal(barrier, inc=1, device_id=(me, dev(yy, xx, c)), device_id_type=MESH)
@@ -70,35 +71,36 @@
         pltpu.make_async_copy(wu_hbm.at[0], wgu.at[:, HID : 2 * HID], w_sem.at[1]),
         pltpu.make_async_copy(wd_hbm.at[0], wd, w_sem.at[2]),
     ]
-    for load in loads:
+    acts = [
+        pltpu.make_async_copy(tok_hbm, ext.at[0:F, 0:TOK], w_sem.at[3]),
+        pltpu.make_async_copy(cot_hbm, ext.at[0:F, TOK : 2 * TOK], w_sem.at[4]),
+    ]
+    for load in acts + loads:
         load.start()
 
-    col = iota((TOK, 256), 1)
-    ids = ids_ref[...]
-    chosen = jnp.where(col < 128, ids[:, 0:1], ids[:, 1:2])
-    member = chosen == col // 16
-    tri = (iota((TOK, TOK), 1) < iota((TOK, TOK), 0)).astype(F32).astype(BF)
-    before = jnp.dot(tri, member.astype(F32).astype(BF), preferred_element_type=F32)
+    row = iota((256, TOK), 0)
+    chosen = jnp.where(row < 128, ids_ref[0:1, :], ids_ref[1:2, :])
+    member = chosen == row // 16
+    tri = (iota((TOK, TOK), 0) < iota((TOK, TOK), 1)).astype(F32).astype(BF)
+    before = jnp.dot(member.astype(F32).astype(BF), tri, preferred_element_type=F32)
     pick = jnp.where(
-        jnp.logical_and(member, before == (col % 8).astype(F32)), 1.0, 0.0
+        jnp.logical_and(member, before == (row % 8).astype(F32)), 1.0, 0.0
     )
-    is_x = (col % 16) < 8
+    is_x = (row % 16) < 8
     pick_out[...] = pick.astype(BF)
     pick2 = jnp.concatenate(
-        [jnp.where(is_x, pick, 0.0), jnp.where(is_x, 0.0, pick)], axis=0
+        [jnp.where(is_x, pick, 0.0), jnp.where(is_x, 0.0, pick)], axis=1
     ).astype(BF)
-    ext[:, 384:512] = jnp.zeros((2 * TOK, 128), BF)
-    ext[0:TOK, 0:F] = tok_ref[...]
-    ext[TOK : 2 * TOK, 0:F] = cot_ref[...]
     gates = gates_ref[...].astype(F32)
-    lane = iota((TOK, 128), 1)
-    ext[0:TOK, 384:512] = jnp.where(
-        lane == 64,
-        gates[:, 0:1],
-        jnp.where(lane == 65, gates[:, 1:2], ext[0:TOK, 384:512].astype(F32)),
+    line = iota((512 - F, TOK), 0)
+    ext[F:512, 0:TOK] = jnp.where(
+        line == 0, gates[0:1, :], jnp.where(line == 1, gates[1:2, :], 0.0)
     ).astype(BF)
+    ext[F:512, TOK : 2 * TOK] = jnp.zeros((512 - F, TOK), BF)
+    for load in acts:
+        load.wait()
     slots = lax.dot_general(
-        pick2, ext[...], (((0,), (0,)), ((), ())), preferred_element_type=F32
+        pick2, ext[...], (((1,), (1,)), ((), ())), preferred_element_type=F32
     ).astype(BF)
     sa[...] = slots[:, 0:256].reshape(NDP, 16, 256)
     sb[...] = slots[:, 256:512].reshape(NDP, 16, 256)
@@ -116,6 +118,7 @@
             )
             copy.start()
             copies.append(copy)
+            started.append(copy)
         dst[pl.ds(me, 1)] = src[pl.ds(me, 1)]
         return copies
 
@@ -135,8 +138,6 @@
 
     def rows(b, lo, n):
         return al.at[pl.ds(pl.multiple_of(b * F + lo, 16), n)]
-
-    sends = []
 
     def push(b, lo, n, to, s):
         copy = pltpu.make_async_remote_copy(
@@ -145,7 +146,7 @@
             device_id=(me, to), device_id_type=MESH,
         )
         copy.start()
-        sends.append(copy)
+        started.append(copy)
 
     def share(b, lo, n, s):
         copy = pltpu.make_async_remote_copy(
@@ -154,7 +155,7 @@
             device_id=(me, sib), device_id_type=MESH,
         )
         copy.start()
-        sends.append(copy)
+        started.append(copy)
 
     def got(b, lo, n, s):
         pltpu.make_async_remote_copy(
@@ -322,6 +323,7 @@
         )
         copy.start()
         ts_copies.append(copy)
+        started.append(copy)
 
     def gate_total(*blocks):
         total = sum(block.astype(F32) for block in blocks)
@@ -343,6 +345,7 @@
             )
             copy.start()
             r_copies.append(copy)
+            started.append(copy)
         else:
             total, gate_sum = part, gate_part
     for n in range(6, -1, -1):
@@ -368,7 +371,7 @@
         copy.wait_recv()
     ret_out[...] = ret[...].reshape(256, 256)
 
-    for copy in copies_a + copies_b + sends + ts_copies + r_copies + b_copies:
+    for copy in started:
         copy.wait_send()
     keep.wait()
 
@@ -385,39 +388,40 @@
 
     @pl.when(pl.program_id(0) == 0)
     def _():
-        col = iota((TOK, 256), 1)
-        is_x = (col % 16) < 8
+        tn = (((0,), (0,)), ((), ()))
+        is_x = (iota((256, TOK), 0) % 16) < 8
         picks = pick[...].astype(F32)
         px = jnp.where(is_x, picks, 0.0).astype(BF)
         pd = jnp.where(is_x, 0.0, picks).astype(BF)
         rows = ret[...]
-        gt_out[:, 0:FA] = jnp.dot(px, rows, preferred_element_type=F32).astype(BF)
-        one = jnp.dot(pd[:, 0:128], rows[0:128], preferred_element_type=F32)
-        two = jnp.dot(pd[:, 128:256], rows[128:256], preferred_element_type=F32)
-        gt_out[:, FA:F] = (one + two)[:, 0:FB].astype(BF)
-        gg_out[:, 0:1] = one[:, FB : FB + 1] + one[:, FB + 1 : FB + 2]
-        gg_out[:, 1:2] = two[:, FB : FB + 1] + two[:, FB + 1 : FB + 2]
+        gt_out[0:FA, :] = lax.dot_general(rows, px, tn, preferred_element_type=F32).astype(BF)
+        one = lax.dot_general(rows[0:128], pd[0:128], tn, preferred_element_type=F32)
+        two = lax.dot_general(rows[128:256], pd[128:256], tn, preferred_element_type=F32)
+        gt_out[FA:F, :] = (one + two)[0:FB].astype(BF)
+        gg_out[0:1, :] = one[FB : FB + 1] + one[FB + 1 : FB + 2]
+        gg_out[1:2, :] = two[FB : FB + 1] + two[FB + 1 : FB + 2]
 
 
 def per_device(tokens, cotangent, gates, expert_ids, w_gate, w_up, w_down):
     vmem = pl.BlockSpec(memory_space=pltpu.VMEM)
     anym = pl.BlockSpec(memory_space=pl.ANY)
+    hbm = pl.BlockSpec(memory_space=pltpu.HBM)
     dma = pltpu.SemaphoreType.DMA
     ret, pick, al, dd, hg = pl.pallas_call(
         comm_kernel,
         out_shape=[
             jax.ShapeDtypeStruct((256, 256), BF),
-            jax.ShapeDtypeStruct((TOK, 256), BF),
+            jax.ShapeDtypeStruct((256, TOK), BF),
             jax.ShapeDtypeStruct((D, 256), BF),
             jax.ShapeDtypeStruct((2 * HID, SLOTS), BF),
             jax.ShapeDtypeStruct((HID, SLOTS), BF),
         ],
-        in_specs=[vmem] * 4 + [anym] * 3,
+        in_specs=[hbm] * 2 + [vmem] * 2 + [hbm] * 3,
         out_specs=[vmem, vmem, anym, vmem, vmem],
         scratch_shapes=[
             pltpu.VMEM((D, 2 * HID), BF),
             pltpu.VMEM((HID, D), BF),
-            pltpu.VMEM((2 * TOK, 512), BF),
+            pltpu.VMEM((512, 2 * TOK), BF),
             pltpu.VMEM((NDP, 16, 256), BF),
             pltpu.VMEM((NDP, 16, 256), BF),
             pltpu.VMEM((NDP, 16, 256), BF),
@@ -434,26 +438,26 @@
             pltpu.VMEM((512, SLOTS), BF),
             pltpu.VMEM((NDP, 16, 256), BF),
             pltpu.VMEM((NDP, 16, 256), BF),
-            dma((3,)), dma(()),
+            dma((5,)), dma(()),
             dma((NDP,)), dma((NDP,)), dma((NDP,)), dma((NDP,)),
             dma((18,)), dma((18,)), dma((20,)), dma((20,)),
             dma((8,)), dma((8,)), dma((7,)), dma((7,)),
             dma((NDP,)), dma((NDP,)),
         ],
         compiler_params=pltpu.CompilerParams(
-            collective_id=0, has_side_effects=True, vmem_limit_bytes=40 * 1024 * 1024
+            collective_id=0, has_side_effects=True, vmem_limit_bytes=58 * 1024 * 1024
         ),
         name="comm",
-    )(tokens, cotangent, expert_ids, gates, w_gate, w_up, w_down)
+    )(tokens.T, cotangent.T, expert_ids.T, gates.T, w_gate, w_up, w_down)
 
     step = 2 * C
     whole = lambda *shape: pl.BlockSpec(shape, lambda i: (0,) * len(shape))
-    return pl.pallas_call(
+    gt, gg, gate, up, down = pl.pallas_call(
         grad_kernel,
         grid=(D // step,),
         out_shape=[
-            jax.ShapeDtypeStruct((TOK, F), BF),
-            jax.ShapeDtypeStruct((TOK, 2), F32),
+            jax.ShapeDtypeStruct((F, TOK), BF),
+            jax.ShapeDtypeStruct((2, TOK), F32),
             jax.ShapeDtypeStruct((1, D, HID), BF),
             jax.ShapeDtypeStruct((1, D, HID), BF),
             jax.ShapeDtypeStruct((1, HID, D), BF),
@@ -463,18 +467,19 @@
             whole(2 * HID, SLOTS),
             whole(HID, SLOTS),
             whole(256, 256),
-            whole(TOK, 256),
+            whole(256, TOK),
         ],
         out_specs=[
-            whole(TOK, F),
-            whole(TOK, 2),
+            whole(F, TOK),
+            whole(2, TOK),
             pl.BlockSpec((1, step, HID), lambda i: (0, i, 0)),
             pl.BlockSpec((1, step, HID), lambda i: (0, i, 0)),
             pl.BlockSpec((1, HID, step), lambda i: (0, 0, i)),
         ],
-        compiler_params=pltpu.CompilerParams(vmem_limit_bytes=32 * 1024 * 1024),
+        compiler_params=pltpu.CompilerParams(vmem_limit_bytes=58 * 1024 * 1024),
         name="grads",
     )(al, dd, hg, ret, pick)
+    return gt.T, gg.T, gate, up, down
 
 
 def solution(mesh):

time: 77.7 us -> 71.5 us (0.920)
  local copies, waits for them, and re-layouts: 9.46 us -> 0 us
  Pallas kernels: 67.4 us -> 70.7 us
    unnamed x10 -> x0, local copies, waits for them, and re-layouts: 8.06 us -> none
    pallas_call x1, Pallas kernels: 4.05 us -> 6.17 us  [per_device(): pl.pallas_call(grad_kernel, grid=(D // step,), out_shape=[jax.ShapeDtypeS...]
    pallas_call x2 -> x0, local copies, waits for them, and re-layouts: 1.4 us -> none  [per_device(): pl.pallas_call(grad_kernel, grid=(D // step,), out_shape=[jax.ShapeDtypeS...]
    pallas_call x1, Pallas kernels: 63.3 us -> 64.5 us  [per_device(): pl.pallas_call(comm_kernel, out_shape=[jax.ShapeDtypeStruct((256, 256), B...]
where the time goes in v2:
time: 71.5 us; the launch traced here: 71.3 us
  Pallas kernels  70.7 us (99%)
    pallas_call x1, Pallas kernels, per_device(): pl.pallas_call(comm_kernel, out_shape=[jax.ShapeDtypeStruct((256, 256), B...  64.5 us
    pallas_call x1, Pallas kernels, per_device(): pl.pallas_call(grad_kernel, grid=(D // step,), out_shape=[jax.ShapeDtypeS...  6.17 us

profile of v2, /device:TPU:1, one launch (start us, length us, event | category | flops | bytes accessed | tf_op | source)
XLA Modules:
  0.0 71.3 jit_solution(16081981576385873185)
XLA Ops:
  0.6 64.5 %comm.1 = (bf16[256,256]{1,0:T(8,128)(2,1)}, bf16[256,128]{1,0:T(8,128)(2,1)}, bf16[7168,256]{1,0:T(8,128)(2,1)}, bf16[256,128]{1,0:T(8,128)(2,1)}, bf16[128,128]{1,0:T(8,128)(2,1)}) custom-call(bf16[448,128]{1,0:T(8,128)(2,1)} %bitcast.6, bf16[448,128]{1,0:T(8,128)(2,1)} %bitcast.7, s32[2,128]{1,0:T(2,128)} %bitcast.8, bf16[2,128]{1,0:T(2,128)(2,1)} %bitcast.9, ...), custom_call_target="tpu_custom_call" | custom-call | tf_op jit(solution)/shard_map/comm/pallas_call | solution.py:410
  65.2 6.2 %grads.1 = (bf16[448,128]{1,0:T(8,128)(2,1)}, f32[2,128]{1,0:T(2,128)}, bf16[1,7168,128]{2,1,0:T(8,128)(2,1)}, bf16[1,7168,128]{2,1,0:T(8,128)(2,1)}, bf16[1,128,7168]{2,1,0:T(8,128)(2,1)}) custom-call(bf16[7168,256]{1,0:T(8,128)(2,1)} %get-tuple-element.15.al, bf16[256,128]{1,0:T(8,128)(2,1)} %get-tuple-element.16.dd, ...), custom_call_target="tpu_custom_call" | custom-call | tf_op jit(solution)/shard_map/grads/pallas_call | solution.py:455

commit v3 on v2

--- a/solution.py
+++ b/solution.py
@@ -24,6 +24,7 @@
 HID = 128
 TOK = 128
 SLOTS = NDP * CAP
+FAR_FIRST = (7, 9, 8, 5, 6, 10, 11, 3, 13, 4, 12, 1, 15, 2, 14)
 RB = F + 16
 
 
@@ -39,10 +40,10 @@
 
 
 def comm_kernel(
-    tok_hbm, cot_hbm, ids_ref, gates_ref, wg_hbm, wu_hbm, wd_hbm,
-    ret_out, pick_out, all_out, dd_out, hg_out,
-    wgu, wd, ext, sa, sb, ra, rb, al, pre, back, dd, hg, tsend, tsib, rsend, rrecv, rpad, retb, ret,
-    w_sem, out_sem, da_send, da_recv, db_send, db_recv, g_send, g_recv, sib_send, sib_recv,
+    tok_hbm, cot_hbm, ids_hbm, gates_hbm, wg_hbm, wu_hbm, wd_hbm,
+    ret_out, pick_out, gate_out, up_out, down_out,
+    ids_ref, gates_ref, wgu, wd, ext, sa, sb, ra, rb, al, pre, back, dd, hg, tsend, tsib, rsend, rrecv, rpad, retb, ret,
+    w_sem, da_send, da_recv, db_send, db_recv, g_send, g_recv, sib_send, sib_recv,
     ts_send, ts_recv, r_send, r_recv, b_send, b_recv,
 ):
     me = lax.axis_index("dp")
@@ -59,7 +60,7 @@
     started = []
 
     barrier = pltpu.get_barrier_semaphore()
-    for i in range(1, NDP):
+    for i in FAR_FIRST:
         pl.semaphore_signal(barrier, inc=1, device_id=((me + i) % NDP, j), device_id_type=MESH)
     chips = [(yy, xx) for yy in (y, yo) for xx in (x, xr, xl, xo)][1:]
     for yy, xx in chips:
@@ -72,11 +73,15 @@
         pltpu.make_async_copy(wd_hbm.at[0], wd, w_sem.at[2]),
     ]
     acts = [
+        pltpu.make_async_copy(ids_hbm, ids_ref, w_sem.at[5]),
+        pltpu.make_async_copy(gates_hbm, gates_ref, w_sem.at[6]),
         pltpu.make_async_copy(tok_hbm, ext.at[0:F, 0:TOK], w_sem.at[3]),
         pltpu.make_async_copy(cot_hbm, ext.at[0:F, TOK : 2 * TOK], w_sem.at[4]),
     ]
     for load in acts + loads:
         load.start()
+    acts[0].wait()
+    acts[1].wait()
 
     row = iota((256, TOK), 0)
     chosen = jnp.where(row < 128, ids_ref[0:1, :], ids_ref[1:2, :])
@@ -97,7 +102,7 @@
         line == 0, gates[0:1, :], jnp.where(line == 1, gates[1:2, :], 0.0)
     ).astype(BF)
     ext[F:512, TOK : 2 * TOK] = jnp.zeros((512 - F, TOK), BF)
-    for load in acts:
+    for load in acts[2:]:
         load.wait()
     slots = lax.dot_general(
         pick2, ext[...], (((1,), (1,)), ((), ())), preferred_element_type=F32
@@ -109,7 +114,7 @@
 
     def dispatch(src, dst, send, recv):
         copies = []
-        for i in range(1, NDP):
+        for i in FAR_FIRST:
             to = (me + i) % NDP
             copy = pltpu.make_async_remote_copy(
                 src_ref=src.at[to], dst_ref=dst.at[me],
@@ -288,9 +293,6 @@
     shared(m_xo, FA + HB, HB, 19)
     forward(yo * 4 + xo)
 
-    keep = pltpu.make_async_copy(al, all_out, out_sem)
-    keep.start()
-
     turned_pre = pre[...].T
     pg, pu = turned_pre[0:HID], turned_pre[HID : 2 * HID]
     sig = jax.nn.sigmoid(pg)
@@ -304,8 +306,8 @@
     dd[0:HID, :] = (dhid * pu * sig * (1.0 + pg * (1.0 - sig))).astype(BF)
     dd[HID : 2 * HID, :] = (dhid * act).astype(BF)
     hg[...] = (hidden * gate_row).astype(BF)
-    dd_out[...] = dd[...]
-    hg_out[...] = hg[...]
+
+    nt = (((1,), (1,)), ((), ()))
 
     def term(b):
         at = pl.ds(pl.multiple_of(b * F, 16), F)
@@ -348,6 +350,20 @@
             started.append(copy)
         else:
             total, gate_sum = part, gate_part
+
+    def grads(i, carry):
+        at = pl.ds(pl.multiple_of(i * C, 128), C)
+        block = al[at, :]
+        both = lax.dot_general(block[:, 0:128], dd[...], nt, preferred_element_type=F32)
+        gate_out[at, :] = both[:, 0:HID].astype(BF)
+        up_out[at, :] = both[:, HID : 2 * HID].astype(BF)
+        down_out[:, at] = lax.dot_general(
+            hg[...], block[:, 128:256], nt, preferred_element_type=F32
+        ).astype(BF)
+        return carry
+
+    lax.fori_loop(0, D // C, grads, 0)
+
     for n in range(6, -1, -1):
         r_copies[n].wait_recv()
         total = total + rrecv[n, 0:F, :].astype(F32)
@@ -373,52 +389,51 @@
 
     for copy in started:
         copy.wait_send()
-    keep.wait()
-
-
-def grad_kernel(al, dd, hg, ret, pick, gt_out, gg_out, gate_out, up_out, down_out):
-    nt = (((1,), (1,)), ((), ()))
-    block = al[...]
-    both = lax.dot_general(block[:, 0:128], dd[...], nt, preferred_element_type=F32)
-    gate_out[0] = both[:, 0:HID].astype(BF)
-    up_out[0] = both[:, HID : 2 * HID].astype(BF)
-    down_out[0] = lax.dot_general(
-        hg[...], block[:, 128:256], nt, preferred_element_type=F32
-    ).astype(BF)
-
-    @pl.when(pl.program_id(0) == 0)
-    def _():
-        tn = (((0,), (0,)), ((), ()))
-        is_x = (iota((256, TOK), 0) % 16) < 8
-        picks = pick[...].astype(F32)
-        px = jnp.where(is_x, picks, 0.0).astype(BF)
-        pd = jnp.where(is_x, 0.0, picks).astype(BF)
-        rows = ret[...]
-        gt_out[0:FA, :] = lax.dot_general(rows, px, tn, preferred_element_type=F32).astype(BF)
-        one = lax.dot_general(rows[0:128], pd[0:128], tn, preferred_element_type=F32)
-        two = lax.dot_general(rows[128:256], pd[128:256], tn, preferred_element_type=F32)
-        gt_out[FA:F, :] = (one + two)[0:FB].astype(BF)
-        gg_out[0:1, :] = one[FB : FB + 1] + one[FB + 1 : FB + 2]
-        gg_out[1:2, :] = two[FB : FB + 1] + two[FB + 1 : FB + 2]
+
+
+def finish_kernel(ret, pick, gate, up, down, gt_out, gg_out, gate_out, up_out, down_out, sems):
+    copies = [
+        pltpu.make_async_copy(gate, gate_out.at[0], sems.at[0]),
+        pltpu.make_async_copy(up, up_out.at[0], sems.at[1]),
+        pltpu.make_async_copy(down, down_out.at[0], sems.at[2]),
+    ]
+    for copy in copies:
+        copy.start()
+    tn = (((0,), (0,)), ((), ()))
+    is_x = (iota((256, TOK), 0) % 16) < 8
+    picks = pick[...].astype(F32)
+    px = jnp.where(is_x, picks, 0.0).astype(BF)
+    pd = jnp.where(is_x, 0.0, picks).astype(BF)
+    rows = ret[...]
+    gt_out[0:FA, :] = lax.dot_general(rows, px, tn, preferred_element_type=F32).astype(BF)
+    one = lax.dot_general(rows[0:128], pd[0:128], tn, preferred_element_type=F32)
+    two = lax.dot_general(rows[128:256], pd[128:256], tn, preferred_element_type=F32)
+    gt_out[FA:F, :] = (one + two)[0:FB].astype(BF)
+    gg_out[0:1, :] = one[FB : FB + 1] + one[FB + 1 : FB + 2]
+    gg_out[1:2, :] = two[FB : FB + 1] + two[FB + 1 : FB + 2]
+    for copy in copies:
+        copy.wait()
 
 
 def per_device(tokens, cotangent, gates, expert_ids, w_gate, w_up, w_down):
     vmem = pl.BlockSpec(memory_space=pltpu.VMEM)
-    anym = pl.BlockSpec(memory_space=pl.ANY)
     hbm = pl.BlockSpec(memory_space=pltpu.HBM)
     dma = pltpu.SemaphoreType.DMA
-    ret, pick, al, dd, hg = pl.pallas_call(
+    operands = (tokens.T, cotangent.T, expert_ids.T, gates.T, w_gate, w_up, w_down)
+    results = pl.pallas_call(
         comm_kernel,
         out_shape=[
-            jax.ShapeDtypeStruct((256, 256), BF),
-            jax.ShapeDtypeStruct((256, TOK), BF),
-            jax.ShapeDtypeStruct((D, 256), BF),
-            jax.ShapeDtypeStruct((2 * HID, SLOTS), BF),
-            jax.ShapeDtypeStruct((HID, SLOTS), BF),
+            pltpu.VMEM((256, 256), BF),
+            pltpu.VMEM((256, TOK), BF),
+            pltpu.VMEM((D, HID), BF),
+            pltpu.VMEM((D, HID), BF),
+            pltpu.VMEM((HID, D), BF),
         ],
-        in_specs=[hbm] * 2 + [vmem] * 2 + [hbm] * 3,
-        out_specs=[vmem, vmem, anym, vmem, vmem],
+        in_specs=[hbm] * 7,
+        out_specs=[vmem] * 5,
         scratch_shapes=[
+            pltpu.VMEM((2, TOK), jnp.int32),
+            pltpu.VMEM((2, TOK), BF),
             pltpu.VMEM((D, 2 * HID), BF),
             pltpu.VMEM((HID, D), BF),
             pltpu.VMEM((512, 2 * TOK), BF),
@@ -438,23 +453,20 @@
             pltpu.VMEM((512, SLOTS), BF),
             pltpu.VMEM((NDP, 16, 256), BF),
             pltpu.VMEM((NDP, 16, 256), BF),
-            dma((5,)), dma(()),
+            dma((7,)),
             dma((NDP,)), dma((NDP,)), dma((NDP,)), dma((NDP,)),
             dma((18,)), dma((18,)), dma((20,)), dma((20,)),
             dma((8,)), dma((8,)), dma((7,)), dma((7,)),
             dma((NDP,)), dma((NDP,)),
         ],
         compiler_params=pltpu.CompilerParams(
-            collective_id=0, has_side_effects=True, vmem_limit_bytes=58 * 1024 * 1024
+            collective_id=0, has_side_effects=True, vmem_limit_bytes=40 * 1024 * 1024
         ),
         name="comm",
-    )(tokens.T, cotangent.T, expert_ids.T, gates.T, w_gate, w_up, w_down)
-
-    step = 2 * C
-    whole = lambda *shape: pl.BlockSpec(shape, lambda i: (0,) * len(shape))
+    )(*(pltpu.with_memory_space_constraint(a, pltpu.HBM) for a in operands))
+
     gt, gg, gate, up, down = pl.pallas_call(
-        grad_kernel,
-        grid=(D // step,),
+        finish_kernel,
         out_shape=[
             jax.ShapeDtypeStruct((F, TOK), BF),
             jax.ShapeDtypeStruct((2, TOK), F32),
@@ -462,23 +474,12 @@
             jax.ShapeDtypeStruct((1, D, HID), BF),
             jax.ShapeDtypeStruct((1, HID, D), BF),
         ],
-        in_specs=[
-            pl.BlockSpec((step, 256), lambda i: (i, 0)),
-            whole(2 * HID, SLOTS),
-            whole(HID, SLOTS),
-            whole(256, 256),
-            whole(256, TOK),
-        ],
-        out_specs=[
-            whole(F, TOK),
-            whole(2, TOK),
-            pl.BlockSpec((1, step, HID), lambda i: (0, i, 0)),
-            pl.BlockSpec((1, step, HID), lambda i: (0, i, 0)),
-            pl.BlockSpec((1, HID, step), lambda i: (0, 0, i)),
-        ],
-        compiler_params=pltpu.CompilerParams(vmem_limit_bytes=58 * 1024 * 1024),
-        name="grads",
-    )(al, dd, hg, ret, pick)
+        in_specs=[vmem] * 5,
+        out_specs=[vmem, vmem, hbm, hbm, hbm],
+        scratch_shapes=[dma((3,))],
+        compiler_params=pltpu.CompilerParams(vmem_limit_bytes=16 * 1024 * 1024),
+        name="finish",
+    )(*(pltpu.with_memory_space_constraint(a, pltpu.VMEM) for a in results))
     return gt.T, gg.T, gate, up, down
 
 

time: 71.5 us -> 65.2 us (0.912)
  Pallas kernels: 70.7 us -> 64.4 us
    pallas_call x2, Pallas kernels: 70.7 us -> 64.4 us  [the longest x1 61.3 us: per_device(): pl.pallas_call(comm_kernel, out_shape=[pltpu.VMEM((256, 256), BF), pltpu....]
where the time goes in v3:
time: 65.2 us; the launch traced here: 65.1 us
  Pallas kernels  64.4 us (99%)
    pallas_call x1, Pallas kernels, per_device(): pl.pallas_call(comm_kernel, out_shape=[pltpu.VMEM((256, 256), BF), pltpu....  61.3 us
    pallas_call x1, Pallas kernels, per_device(): pl.pallas_call(finish_kernel, out_shape=[jax.ShapeDtypeStruct((F, TOK), B...  3.12 us

profile of v3, /device:TPU:1, one launch (start us, length us, event | category | flops | bytes accessed | tf_op | source)
XLA Modules:
  0.0 65.1 jit_solution(2509378903150246799)
XLA Ops:
  0.6 61.3 %comm.1 = (bf16[256,256]{1,0:T(8,128)(2,1)S(1)}, bf16[256,128]{1,0:T(8,128)(2,1)S(1)}, bf16[7168,128]{1,0:T(8,128)(2,1)S(1)}, bf16[7168,128]{1,0:T(8,128)(2,1)S(1)}, bf16[128,7168]{1,0:T(8,128)(2,1)S(1)}) custom-call(bf16[448,128]{1,0:T(8,128)(2,1)} %bitcast.6, bf16[448,128]{1,0:T(8,128)(2,1)} %bitcast.7, s32[2,128]{1,0:T(2,128)} %bitcast.8, ...), custom_call_target="tpu_custom_call" | custom-call | tf_op jit(solution)/shard_map/comm/pallas_call | solution.py:423
  62.0 3.1 %finish.1 = (bf16[448,128]{1,0:T(8,128)(2,1)}, f32[2,128]{1,0:T(2,128)}, bf16[1,7168,128]{2,1,0:T(8,128)(2,1)}, bf16[1,7168,128]{2,1,0:T(8,128)(2,1)}, bf16[1,128,7168]{2,1,0:T(8,128)(2,1)}) custom-call(bf16[256,256]{1,0:T(8,128)(2,1)S(1)} %get-tuple-element.15.ret, bf16[256,128]{1,0:T(8,128)(2,1)S(1)} %get-tuple-element.16.pick, ...), custom_call_target="tpu_custom_call" | custom-call | tf_op jit(solution)/shard_map/finish/pallas_call | solution.py:468

commit v4 on v0

v4 whole, which is shorter than its diff:
```python
import functools

import jax
import jax.numpy as jnp
from jax import lax
from jax.experimental import pallas as pl
from jax.experimental.pallas import tpu as pltpu
from jax.sharding import PartitionSpec as P

MESH = pl.DeviceIdType.MESH
BF = jnp.bfloat16
F32 = jnp.float32

CAP = 8
NDP = 16
NEX = 16
F = 448
FA = 256
FB = F - FA
HB = FB // 2
HA = FA // 2
C = 2 * F
D = NEX * F
HID = 128
TOK = 128
SLOTS = NDP * CAP
NEAR = (0, 2, 14, 4, 12, 6, 10, 1)
FAR = (8, 7, 9, 11, 5, 13, 3, 15)
OFFSETS = NEAR + FAR
FH = F // 2
RB = FH + 16


def iota(shape, dim):
    return lax.broadcasted_iota(jnp.int32, shape, dim)


def split_gate(row):
    hi = row.astype(BF).astype(F32)
    lo = row - hi
    r = iota((16, row.shape[1]), 0)
    return jnp.where(r == 0, hi, jnp.where(r == 1, lo, 0.0)).astype(BF)


def comm_kernel(
    tok_hbm, cot_hbm, ids_hbm, gates_hbm, wg_hbm, wu_hbm, wd_hbm,
    ret_out, pick_out, gate_out, up_out, down_out,
    ids_ref, gates_ref, wgu, wd, ext, sx, rx, al0, al1, pre, back, dd, hg,
    tsend, tsib, rsend, rrecv, rpad, retb, ret,
    w_sem, d_send, d_recv, g_send, g_recv, sib_send, sib_recv,
    ts_send, ts_recv, r_send, r_recv, b_send, b_recv,
):
    me = lax.axis_index("dp")
    j = lax.axis_index("expert")
    y, x, c = j // 8, (j // 2) % 4, j % 2

    def dev(yy, xx, cc):
        return yy * 8 + xx * 2 + cc

    xr, xl, xo = (x + 1) % 4, (x + 3) % 4, (x + 2) % 4
    yo = 1 - y
    sib, xp, xm, yp = dev(y, x, 1 - c), dev(y, xr, c), dev(y, xl, c), dev(yo, x, c)

    started = []

    barrier = pltpu.get_barrier_semaphore()
    for i in FAR + NEAR[:0:-1]:
        pl.semaphore_signal(barrier, inc=1, device_id=((me + i) % NDP, j), device_id_type=MESH)
    chips = [(yy, xx) for yy in (y, yo) for xx in (x, xr, xl, xo)][1:]
    for yy, xx in chips:
        pl.semaphore_signal(barrier, inc=1, device_id=(me, dev(yy, xx, c)), device_id_type=MESH)
    pl.semaphore_signal(barrier, inc=1, device_id=(me, sib), device_id_type=MESH)

    loads = [
        pltpu.make_async_copy(wg_hbm.at[0], wgu.at[:, 0:HID], w_sem.at[0]),
        pltpu.make_async_copy(wu_hbm.at[0], wgu.at[:, HID : 2 * HID], w_sem.at[1]),
        pltpu.make_async_copy(wd_hbm.at[0], wd, w_sem.at[2]),
    ]
    acts = [
        pltpu.make_async_copy(ids_hbm, ids_ref, w_sem.at[5]),
        pltpu.make_async_copy(gates_hbm, gates_ref, w_sem.at[6]),
        pltpu.make_async_copy(tok_hbm, ext.at[0:F, 0:TOK], w_sem.at[3]),
        pltpu.make_async_copy(cot_hbm, ext.at[0:F, TOK : 2 * TOK], w_sem.at[4]),
    ]
    for load in acts + loads:
        load.start()
    acts[0].wait()
    acts[1].wait()

    row = iota((256, TOK), 0)
    ahead = sum(jnp.where(row // 16 == n, o, 0) for n, o in enumerate(OFFSETS))
    expert = (ahead + me) % NDP
    in_first = expert < NDP // 2
    member = jnp.where(in_first, ids_ref[0:1, :], ids_ref[1:2, :]) == expert
    tri = (iota((TOK, TOK), 0) < iota((TOK, TOK), 1)).astype(F32).astype(BF)
    before = jnp.dot(member.astype(F32).astype(BF), tri, preferred_element_type=F32)
    pick = jnp.where(
        jnp.logical_and(member, before == (row % 8).astype(F32)), 1.0, 0.0
    )
    is_x = (row % 16) < 8
    pick_x = jnp.where(is_x, pick, 0.0)
    pick_d = jnp.where(is_x, 0.0, pick)
    pick_out[0] = jnp.where(in_first, pick_x, 0.0).astype(BF)
    pick_out[1] = jnp.where(in_first, 0.0, pick_x).astype(BF)
    pick_out[2] = pick_d.astype(BF)
    gates = gates_ref[...].astype(F32)
    line = iota((512 - F, TOK), 0)
    ext[F:512, 0:TOK] = jnp.where(
        line == 0, gates[0:1, :], jnp.where(line == 1, gates[1:2, :], 0.0)
    ).astype(BF)
    ext[F:512, TOK : 2 * TOK] = jnp.zeros((512 - F, TOK), BF)
    for load in acts[2:]:
        load.wait()
    slots = lax.dot_general(
        jnp.concatenate([pick_x, pick_d], axis=1).astype(BF), ext[...],
        (((1,), (1,)), ((), ())), preferred_element_type=F32,
    ).astype(BF)
    sx[...] = slots.reshape(NDP, 16, 512)
    rx[0] = sx[0]

    r = iota((128, 128), 0)
    k = iota((128, 128), 1)
    perm = jnp.where(k == ((r % 16) // 8) * 64 + (r // 16) * 8 + r % 8, 1.0, 0.0).astype(BF)
    nt = (((1,), (1,)), ((), ()))
    pre[...] = jnp.zeros_like(pre)
    back[...] = jnp.zeros_like(back)

    pl.semaphore_wait(barrier, NDP - 1 + len(chips) + 1)

    d_copies = [None]
    for n, o in enumerate(OFFSETS):
        if o:
            copy = pltpu.make_async_remote_copy(
                src_ref=sx.at[n], dst_ref=rx.at[n],
                send_sem=d_send.at[n], recv_sem=d_recv.at[n],
                device_id=((me + o) % NDP, j), device_id_type=MESH,
            )
            copy.start()
            d_copies.append(copy)
            started.append(copy)

    al = (al0, al1)

    def piece(h, b, lo, n):
        return al[h].at[pl.ds(pl.multiple_of(b * F + lo, 16), n)]

    def move(h, b, lo, n, to, s, sems):
        ref = piece(h, b, lo, n)
        return pltpu.make_async_remote_copy(
            src_ref=ref, dst_ref=ref,
            send_sem=sems[0].at[h, s], recv_sem=sems[1].at[h, s],
            device_id=(me, to), device_id_type=MESH,
        )

    def push(h, b, lo, n, to, s):
        copy = move(h, b, lo, n, to, s, (g_send, g_recv))
        copy.start()
        started.append(copy)

    def share(h, b, lo, n, s):
        copy = move(h, b, lo, n, sib, s, (sib_send, sib_recv))
        copy.start()
        started.append(copy)

    def got(h, b, lo, n, s):
        move(h, b, lo, n, sib, s, (g_send, g_recv)).wait_recv()

    def shared(h, b, lo, n, s):
        move(h, b, lo, n, sib, s, (sib_send, sib_recv)).wait_recv()

    def forward(h, chip):
        at = pl.ds(pl.multiple_of(chip * C, 128), C)
        block = al[h][at, :]
        pre[h] += lax.dot_general(
            block, wgu[at, :], (((0,), (0,)), ((), ())), preferred_element_type=F32
        )
        back[h] += jnp.dot(wd[:, at], block, preferred_element_type=F32)

    gate_rows = [None, None]

    def gather_steps(h):
        b_own, b_xr, b_xl, b_xo = (dev(y, xx, c) for xx in (x, xr, xl, xo))
        o_own, o_xr, o_xl, o_xo = (dev(yo, xx, c) for xx in (x, xr, xl, xo))
        n_own, n_xr, n_xl, n_xo = (dev(y, xx, 1 - c) for xx in (x, xr, xl, xo))
        m_own, m_xr, m_xl, m_xo = (dev(yo, xx, 1 - c) for xx in (x, xr, xl, xo))

        def own():
            for n in range(8 * h, 8 * h + 8):
                if d_copies[n] is not None:
                    d_copies[n].wait_recv()
            turned = lax.dot_general(
                rx[8 * h : 8 * h + 8].reshape(128, 512), perm,
                (((0,), (0,)), ((), ())), preferred_element_type=F32,
            )
            al[h][pl.ds(pl.multiple_of(j * F, 16), F), :] = turned[0:F].astype(BF)
            gate_rows[h] = jnp.where(
                me < NDP // 2, turned[F : F + 1], turned[F + 1 : F + 2]
            )
            push(h, b_own, 0, FA, yp, 0)
            push(h, b_own, 0, FA, xp, 1)
            push(h, b_own, 0, FA, xm, 2)
            push(h, b_own, FA, FB, xp, 4)
            push(h, b_own, FA, FB, xm, 5)
            push(h, b_own, FA, FB, yp, 3)
            share(h, b_own, 0, FA, 0)
            share(h, b_own, FA, FB, 1)

        def first_y():
            got(h, o_own, 0, FA, 0)
            push(h, o_own, 0, FA, xp, 6)
            push(h, o_own, 0, FA, xm, 7)
            share(h, o_own, 0, FA, 2)

        def first_x():
            got(h, b_xl, 0, FA, 1)
            push(h, b_xl, 0, HA, xp, 12)
            share(h, b_xl, 0, FA, 5)
            got(h, b_xr, 0, FA, 2)
            push(h, b_xr, HA, HA, xm, 13)
            share(h, b_xr, 0, FA, 6)

        def second_x():
            got(h, b_xl, FA, FB, 4)
            push(h, b_xl, FA, HB, xp, 8)
            push(h, b_xl, FA, FB, yp, 9)
            share(h, b_xl, FA, FB, 3)
            got(h, b_xr, FA, FB, 5)
            push(h, b_xr, FA + HB, HB, xm, 10)
            push(h, b_xr, FA, FB, yp, 11)
            share(h, b_xr, FA, FB, 4)

        def work_own():
            if h == 0:
                for load in loads:
                    load.wait()
            shared(h, n_own, 0, FA, 0)
            shared(h, n_own, FA, FB, 1)
            forward(h, y * 4 + x)

        def second_y():
            got(h, o_own, FA, FB, 3)
            share(h, o_own, FA, FB, 11)

        def first_yx():
            got(h, o_xl, 0, FA, 6)
            push(h, o_xl, 0, HA, xp, 16)
            share(h, o_xl, 0, FA, 9)
            got(h, o_xr, 0, FA, 7)
            push(h, o_xr, HA, HA, xm, 17)
            share(h, o_xr, 0, FA, 10)

        def work_x():
            shared(h, n_xl, FA, FB, 3)
            shared(h, n_xl, 0, FA, 5)
            forward(h, y * 4 + xl)
            shared(h, n_xr, FA, FB, 4)
            shared(h, n_xr, 0, FA, 6)
            forward(h, y * 4 + xr)

        def second_xx():
            got(h, b_xo, FA, HB, 8)
            push(h, b_xo, FA, HB, yp, 14)
            share(h, b_xo, FA, HB, 7)
            got(h, b_xo, FA + HB, HB, 10)
            push(h, b_xo, FA + HB, HB, yp, 15)
            share(h, b_xo, FA + HB, HB, 8)

        def second_xy():
            got(h, o_xl, FA, FB, 9)
            share(h, o_xl, FA, FB, 12)
            got(h, o_xr, FA, FB, 11)
            share(h, o_xr, FA, FB, 13)

        def work_y():
            shared(h, m_own, 0, FA, 2)
            shared(h, m_own, FA, FB, 11)
            forward(h, yo * 4 + x)

        def first_xx():
            got(h, b_xo, 0, HA, 12)
            share(h, b_xo, 0, HA, 14)
            got(h, b_xo, HA, HA, 13)
            share(h, b_xo, HA, HA, 15)

        def work_xy():
            shared(h, m_xl, 0, FA, 9)
            shared(h, m_xl, FA, FB, 12)
            forward(h, yo * 4 + xl)
            shared(h, m_xr, 0, FA, 10)
            shared(h, m_xr, FA, FB, 13)
            forward(h, yo * 4 + xr)

        def work_xx():
            shared(h, n_xo, FA, HB, 7)
            shared(h, n_xo, FA + HB, HB, 8)
            shared(h, n_xo, 0, HA, 14)
            shared(h, n_xo, HA, HA, 15)
            forward(h, y * 4 + xo)

        def last():
            got(h, o_xo, 0, HA, 16)
            share(h, o_xo, 0, HA, 16)
            got(h, o_xo, HA, HA, 17)
            share(h, o_xo, HA, HA, 17)
            got(h, o_xo, FA, HB, 14)
            share(h, o_xo, FA, HB, 18)
            got(h, o_xo, FA + HB, HB, 15)
            share(h, o_xo, FA + HB, HB, 19)

        def work_last():
            shared(h, m_xo, 0, HA, 16)
            shared(h, m_xo, HA, HA, 17)
            shared(h, m_xo, FA, HB, 18)
            shared(h, m_xo, FA + HB, HB, 19)
            forward(h, yo * 4 + xo)

        return [
            (0.0, own), (3.9, first_y), (4.0, first_x), (5.0, second_x), (6.0, work_own),
            (7.5, second_y), (8.0, first_yx), (8.6, work_x), (9.0, second_xx), (9.3, second_xy),
            (9.4, work_y), (9.9, first_xx), (10.5, work_xy), (11.2, work_xx), (11.9, last),
            (13.0, work_last),
        ]

    gate_terms = [None, None]

    def units(h):
        turned_pre = pre[h].T
        pg, pu = turned_pre[0:HID], turned_pre[HID : 2 * HID]
        sig = jax.nn.sigmoid(pg)
        act = pg * sig
        hidden = act * pu
        bk = pltpu.roll(back[h], 64, 1)
        ok = iota((HID, 128), 1) < 64
        gate_terms[h] = split_gate(
            jnp.sum(
                jnp.where(ok, bk * hidden.astype(BF).astype(F32), 0.0), axis=0, keepdims=True
            )
        )
        dhid = gate_rows[h] * bk
        dg = jnp.where(ok, dhid * pu * sig * (1.0 + pg * (1.0 - sig)), 0.0)
        du = jnp.where(ok, dhid * act, 0.0)
        dd[h, 0:HID, :] = dg.astype(BF)
        dd[h, HID : 2 * HID, :] = du.astype(BF)
        dd[h, 2 * HID : 3 * HID, :] = pltpu.roll(dg, 64, 1).astype(BF)
        dd[h, 3 * HID : 4 * HID, :] = pltpu.roll(du, 64, 1).astype(BF)
        hg[h] = pltpu.roll(jnp.where(ok, hidden * gate_rows[h], 0.0), 64, 1).astype(BF)

    def term(h, b):
        lo = wgu[pl.ds(pl.multiple_of(b * F, 16), FH), :]
        hi = wgu[pl.ds(pl.multiple_of(b * F + FH, 16), FH), :]
        return jnp.dot(lo, dd[h, 0 : 2 * HID, :], preferred_element_type=F32) + jnp.dot(
            hi, dd[h, 2 * HID : 4 * HID, :], preferred_element_type=F32
        )

    def gate_total(*blocks):
        total = sum(block.astype(F32) for block in blocks)
        return jnp.sum(total, axis=0, keepdims=True)

    order = [(yo, xo), (yo, xl), (yo, xr), (y, xo), (yo, x), (y, xl), (y, xr), (y, x)]
    ts_copies = ([], [])
    r_copies = ([], [])
    mine = [None, None]

    def to_sibling(h):
        for n, (yy, xx) in enumerate(order):
            tsend[h, n, 0:FH, :] = term(h, dev(yy, xx, 1 - c)).astype(BF)
            tsend[h, n, FH:RB, :] = gate_terms[h]
            copy = pltpu.make_async_remote_copy(
                src_ref=tsend.at[h, n], dst_ref=tsib.at[h, n],
                send_sem=ts_send.at[h, n], recv_sem=ts_recv.at[h, n],
                device_id=(me, sib), device_id_type=MESH,
            )
            copy.start()
            ts_copies[h].append(copy)
            started.append(copy)

    def to_chips(h):
        for n, (yy, xx) in enumerate(order):
            part = term(h, dev(yy, xx, c))
            ts_copies[h][n].wait_recv()
            part = part + tsib[h, n, 0:FH, :].astype(F32)
            gate_part = gate_total(gate_terms[h], tsib[h, n, FH:RB, :])
            if n < 7:
                rsend[h, n, 0:FH, :] = part.astype(BF)
                rsend[h, n, FH:RB, :] = split_gate(gate_part)
                copy = pltpu.make_async_remote_copy(
                    src_ref=rsend.at[h, n], dst_ref=rrecv.at[h, n],
                    send_sem=r_send.at[h, n], recv_sem=r_recv.at[h, n],
                    device_id=(me, dev(yy, xx, c)), device_id_type=MESH,
                )
                copy.start()
                r_copies[h].append(copy)
                started.append(copy)
            else:
                mine[h] = (part, gate_part)

    b_copies = [None]

    def give_back(h):
        total, gate_sum = mine[h]
        for n in range(6, -1, -1):
            r_copies[h][n].wait_recv()
            total = total + rrecv[h, n, 0:FH, :].astype(F32)
            gate_sum = gate_sum + gate_total(rrecv[h, n, FH:RB, :])
        rpad[0:FH, :] = total.astype(BF)
        rpad[FH:RB, :] = split_gate(gate_sum)
        rpad[RB:256, :] = jnp.zeros((256 - RB, 128), BF)
        rows = lax.dot_general(perm, rpad[...], nt, preferred_element_type=F32)
        retb[8 * h : 8 * h + 8] = rows.astype(BF).reshape(8, 16, 256)
        for n in range(8 * h, 8 * h + 8):
            o = OFFSETS[n]
            if o:
                copy = pltpu.make_async_remote_copy(
                    src_ref=retb.at[n], dst_ref=ret.at[n],
                    send_sem=b_send.at[n], recv_sem=b_recv.at[n],
                    device_id=((me + NDP - o) % NDP, j), device_id_type=MESH,
                )
                copy.start()
                b_copies.append(copy)
                started.append(copy)
            else:
                ret[0] = retb[0]

    def grads(i, carry):
        at = pl.ds(pl.multiple_of(i * C, 128), C)
        near, far = al0[at, :], al1[at, :]
        both = lax.dot_general(near, dd[0, 0 : 2 * HID, :], nt, preferred_element_type=F32)
        both += lax.dot_general(far, dd[1, 0 : 2 * HID, :], nt, preferred_element_type=F32)
        gate_out[at, :] = both[:, 0:HID].astype(BF)
        up_out[at, :] = both[:, HID : 2 * HID].astype(BF)
        down = lax.dot_general(hg[0], near, nt, preferred_element_type=F32)
        down += lax.dot_general(hg[1], far, nt, preferred_element_type=F32)
        down_out[:, at] = down.astype(BF)
        return carry

    steps = [(1.2 * t, step) for t, step in gather_steps(0)]
    steps += [(2.5 + 1.05 * t, step) for t, step in gather_steps(1)]
    steps += [
        (16.35, functools.partial(units, 1)),
        (16.45, functools.partial(to_sibling, 1)),
        (17.85, functools.partial(to_chips, 1)),
        (17.96, functools.partial(units, 0)),
        (17.97, functools.partial(to_sibling, 0)),
        (17.98, functools.partial(to_chips, 0)),
        (20.0, lambda: lax.fori_loop(0, 2, grads, 0)),
        (21.0, functools.partial(give_back, 1)),
        (22.0, lambda: lax.fori_loop(2, D // C, grads, 0)),
        (24.0, functools.partial(give_back, 0)),
    ]
    for _, step in sorted(steps, key=lambda pair: pair[0]):
        step()

    for copy in b_copies[1:]:
        copy.wait_recv()
    ret_out[...] = ret[...].reshape(256, 256)
    for copy in started:
        copy.wait_send()


def finish_kernel(ret, pick, gate, up, down, gt_out, gg_out, gate_out, up_out, down_out, sems):
    copies = [
        pltpu.make_async_copy(gate, gate_out.at[0], sems.at[0]),
        pltpu.make_async_copy(up, up_out.at[0], sems.at[1]),
        pltpu.make_async_copy(down, down_out.at[0], sems.at[2]),
    ]
    for copy in copies:
        copy.start()
    tn = (((0,), (0,)), ((), ()))
    rows = ret[...]
    one, two, low = (
        lax.dot_general(rows, pick[n], tn, preferred_element_type=F32) for n in range(3)
    )
    gt_out[0:FH, :] = (one + two)[0:FH].astype(BF)
    gt_out[FH:F, :] = low[0:FH].astype(BF)
    gg_out[0:1, :] = one[FH : FH + 1] + one[FH + 1 : FH + 2]
    gg_out[1:2, :] = two[FH : FH + 1] + two[FH + 1 : FH + 2]
    for copy in copies:
        copy.wait()


def per_device(tokens, cotangent, gates, expert_ids, w_gate, w_up, w_down):
    vmem = pl.BlockSpec(memory_space=pltpu.VMEM)
    hbm = pl.BlockSpec(memory_space=pltpu.HBM)
    dma = pltpu.SemaphoreType.DMA
    operands = (tokens.T, cotangent.T, expert_ids.T, gates.T, w_gate, w_up, w_down)
    results = pl.pallas_call(
        comm_kernel,
        out_shape=[
            pltpu.VMEM((256, 256), BF),
            pltpu.VMEM((3, 256, TOK), BF),
            pltpu.VMEM((D, HID), BF),
            pltpu.VMEM((D, HID), BF),
            pltpu.VMEM((HID, D), BF),
        ],
        in_specs=[hbm] * 7,
        out_specs=[vmem] * 5,
        scratch_shapes=[
            pltpu.VMEM((2, TOK), jnp.int32),
            pltpu.VMEM((2, TOK), BF),
            pltpu.VMEM((D, 2 * HID), BF),
            pltpu.VMEM((HID, D), BF),
            pltpu.VMEM((512, 2 * TOK), BF),
            pltpu.VMEM((NDP, 16, 512), BF),
            pltpu.VMEM((NDP, 16, 512), BF),
            pltpu.VMEM((D, 128), BF),
            pltpu.VMEM((D, 128), BF),
            pltpu.VMEM((2, 128, 2 * HID), F32),
            pltpu.VMEM((2, HID, 128), F32),
            pltpu.VMEM((2, 4 * HID, 128), BF),
            pltpu.VMEM((2, HID, 128), BF),
            pltpu.VMEM((2, 8, RB, 128), BF),
            pltpu.VMEM((2, 8, RB, 128), BF),
            pltpu.VMEM((2, 7, RB, 128), BF),
            pltpu.VMEM((2, 7, RB, 128), BF),
            pltpu.VMEM((256, 128), BF),
            pltpu.VMEM((NDP, 16, 256), BF),
            pltpu.VMEM((NDP, 16, 256), BF),
            dma((7,)),
            dma((NDP,)), dma((NDP,)),
            dma((2, 18)), dma((2, 18)), dma((2, 20)), dma((2, 20)),
            dma((2, 8)), dma((2, 8)), dma((2, 7)), dma((2, 7)),
            dma((NDP,)), dma((NDP,)),
        ],
        compiler_params=pltpu.CompilerParams(
            collective_id=0, has_side_effects=True, vmem_limit_bytes=40 * 1024 * 1024
        ),
        name="comm",
    )(*(pltpu.with_memory_space_constraint(a, pltpu.HBM) for a in operands))

    gt, gg, gate, up, down = pl.pallas_call(
        finish_kernel,
        out_shape=[
            jax.ShapeDtypeStruct((F, TOK), BF),
            jax.ShapeDtypeStruct((2, TOK), F32),
            jax.ShapeDtypeStruct((1, D, HID), BF),
            jax.ShapeDtypeStruct((1, D, HID), BF),
            jax.ShapeDtypeStruct((1, HID, D), BF),
        ],
        in_specs=[vmem] * 5,
        out_specs=[vmem, vmem, hbm, hbm, hbm],
        scratch_shapes=[dma((3,))],
        compiler_params=pltpu.CompilerParams(vmem_limit_bytes=16 * 1024 * 1024),
        name="finish",
    )(*(pltpu.with_memory_space_constraint(a, pltpu.VMEM) for a in results))
    return gt.T, gg.T, gate, up, down


def solution(mesh):
    in_specs = (
        P("dp", "expert"),
        P("dp", "expert"),
        P("dp", None),
        P("dp", None),
        P("dp", None, "expert"),
        P("dp", None, "expert"),
        P("dp", "expert", None),
    )
    out_specs = (
        P("dp", "expert"),
        P("dp", None),
        P("dp", None, "expert"),
        P("dp", None, "expert"),
        P("dp", "expert", None),
    )
    return jax.shard_map(
        per_device, mesh=mesh, in_specs=in_specs, out_specs=out_specs, check_vma=False
    )
```

time: 322 us -> 61.4 us (0.19); the launches traced: 318 us -> 61.3 us
  waiting for transfers between devices: 145 us -> 0 us
  blocking collectives: 72.3 us -> 0 us
  Pallas kernels: 0 us -> 60.7 us
  local copies, waits for them, and re-layouts: 49.9 us -> 0 us
  starting transfers between devices: 18.3 us -> 0 us
  matrix products: 17.3 us -> 0 us
  between operations: 14 us -> 0.64 us
    all_gather x2 -> x0, waiting for transfers between devices: 123 us -> none  [the longest x1 68.3 us: per_device(): lax.all_gather(slot_d, 'expert', axis=2, tiled=True)]
    pallas_call x0 -> x2, Pallas kernels: none -> 60.7 us  [the longest x1 57.5 us: per_device(): pl.pallas_call(comm_kernel, out_shape=[pltpu.VMEM((256, 256), BF), pltpu....]
    all_to_all x3 -> x0, blocking collectives: 45.6 us -> none  [the longest x1 21.5 us: per_device(): lax.all_to_all(slot_x, 'dp', split_axis=0, concat_axis=0, tiled=True)]
    all_gather x2 -> x0, local copies, waits for them, and re-layouts: 30.4 us -> none  [the longest x1 15.2 us: per_device(): lax.all_gather(slot_x, 'expert', axis=2, tiled=True)]
    psum x1 -> x0, blocking collectives: 26.8 us -> none  [per_device(): gate_back = lax.psum(gate_part, 'expert').reshape(1, experts, CAP)]
    all_to_all x2 -> x0, starting transfers between devices: 18.2 us -> none  [the longest x1 9.16 us: per_device(): lax.all_to_all(gate_back.astype(jnp.bfloat16), 'dp', split_axis=1, concat...]
    dot_general x10 -> x0, matrix products: 17.3 us -> none  [the longest x1 3.56 us: per_device(): lax.dot_general(x_all, d_gate, (((0,), (0,)), ((), ())), preferred_elemen...]
    unnamed x4 -> x0, waiting for transfers between devices: 11.6 us -> none
  transfers between devices with their start and end apart: 5 -> 0, of which waited for: 5 -> 0; matrix products, arithmetic and copies ran while one was open for 11% -> 0% of each run, Pallas kernels for 0% -> 0%
where the time goes in v4:
time: 61.4 us; the launch traced here: 61.3 us
  Pallas kernels  60.7 us (99%)
  between operations  0.64 us (1%)
    pallas_call x1, Pallas kernels, per_device(): pl.pallas_call(comm_kernel, out_shape=[pltpu.VMEM((256, 256), BF), pltpu....  57.5 us
    pallas_call x1, Pallas kernels, per_device(): pl.pallas_call(finish_kernel, out_shape=[jax.ShapeDtypeStruct((F, TOK), B...  3.14 us

profile of v4, /device:TPU:1, one launch (start us, length us, event | category | flops | bytes accessed | tf_op | source)
XLA Modules:
  0.0 61.3 jit_solution(8613453905171395986)
XLA Ops:
  0.6 57.5 %comm.1 = (bf16[256,256]{1,0:T(8,128)(2,1)S(1)}, bf16[3,256,128]{2,1,0:T(8,128)(2,1)S(1)}, bf16[7168,128]{1,0:T(8,128)(2,1)S(1)}, bf16[7168,128]{1,0:T(8,128)(2,1)S(1)}, bf16[128,7168]{1,0:T(8,128)(2,1)S(1)}) custom-call(bf16[448,128]{1,0:T(8,128)(2,1)} %bitcast.6, bf16[448,128]{1,0:T(8,128)(2,1)} %bitcast.7, s32[2,128]{1,0:T(2,128)} %bitcast.8, ...), custom_call_target="tpu_custom_call" | custom-call | tf_op jit(solution)/shard_map/comm/pallas_call | solution.py:486
  58.2 3.1 %finish.1 = (bf16[448,128]{1,0:T(8,128)(2,1)}, f32[2,128]{1,0:T(2,128)}, bf16[1,7168,128]{2,1,0:T(8,128)(2,1)}, bf16[1,7168,128]{2,1,0:T(8,128)(2,1)}, bf16[1,128,7168]{2,1,0:T(8,128)(2,1)}) custom-call(bf16[256,256]{1,0:T(8,128)(2,1)S(1)} %get-tuple-element.15.ret, bf16[3,256,128]{2,1,0:T(8,128)(2,1)S(1)} %get-tuple-element.16.pick, ...), custom_call_target="tpu_custom_call" | custom-call | tf_op jit(solution)/shard_map/finish/pallas_call | solution.py:530

commit v5 on v4

v5 whole, which is shorter than its diff:
```python
import functools

import jax
import jax.numpy as jnp
from jax import lax
from jax.experimental import pallas as pl
from jax.experimental.pallas import tpu as pltpu
from jax.sharding import PartitionSpec as P

MESH = pl.DeviceIdType.MESH
BF = jnp.bfloat16
F32 = jnp.float32

CAP = 8
NDP = 16
NEX = 16
F = 448
FA = 256
FB = F - FA
HB = FB // 2
HA = FA // 2
C = 2 * F
D = NEX * F
HID = 128
TOK = 128
SLOTS = NDP * CAP
NEAR = (0, 2, 14, 4, 12, 6, 10, 1)
FAR = (8, 7, 9, 11, 5, 13, 3, 15)
OFFSETS = NEAR + FAR
FH = F // 2
YR = 144
RB = FH + 16

ORDER = (
    "0own 0Wown 1own 0Aoo", "0Bxl 0Bxr 0Axl 0Axr", "0Boo 1Wown 0Wxl 0Wxr",
    "1Bxl 1Bxr 1Aoo 0Woo", "1Axl 1Axr 1Boo 0Boxl", "1Wxl 1Wxr 1Woo 0Bxo1",
    "0Bxo2 0Aoxl 0Aoxr 0Boxr", "0Axo1 0Axo2 1Bxo1 1Bxo2", "1Boxl 0Woxl 0Woxr 1Boxr",
    "0Wxo 1Aoxl 1Aoxr 0Boxo1", "1Axo1 1Axo2 0Boxo2 1Boxo1", "0Aoxo1 0Aoxo2 1Woxl 1Boxo2",
    "1Woxr 1Wxo 0Woxo 1Aoxo1", "1Aoxo2 0U 1Woxo 1U", "0T0 0T1 0T2 0T3",
    "0T4 0T5 0T6 0T7", "0C0 0C1 0C2 0C3", "0C4 0C5 0C6 0C7",
    "0N0 0N1 0N2 0N3", "0N4 0N5 0N6 0N7", "1P2xo 1P2xr 1P2xl 1Q2",
    "0P2xo 0P2xr 0P2xl 0Q2", "0G02 1B 0B 0G28",
)


def iota(shape, dim):
    return lax.broadcasted_iota(jnp.int32, shape, dim)


def split_gate(row):
    hi = row.astype(BF).astype(F32)
    lo = row - hi
    r = iota((16, row.shape[1]), 0)
    return jnp.where(r == 0, hi, jnp.where(r == 1, lo, 0.0)).astype(BF)


def comm_kernel(
    tok_hbm, cot_hbm, ids_hbm, gates_hbm, wg_hbm, wu_hbm, wd_hbm,
    ret_out, pick_out, gate_out, up_out, down_out,
    ids_ref, gates_ref, wgu, wt, ext, sx, rx, al0, al1, acc, dd, hg,
    tsend, tsib, y_keep, y_send, y_recv, yx_send, yx_recv, x_keep, x_send, x_recv, xy_send, xy_recv,
    rpad, retb, ret,
    w_sem, d_send, d_recv, g_send, g_recv, sib_send, sib_recv,
    ts_send, ts_recv, ys_sem, yr_sem, yxs_sem, yxr_sem, xs_sem, xr_sem, xys_sem, xyr_sem,
    b_send, b_recv,
):
    me = lax.axis_index("dp")
    j = lax.axis_index("expert")
    y, x, c = j // 8, (j // 2) % 4, j % 2

    def dev(yy, xx, cc):
        return yy * 8 + xx * 2 + cc

    xr, xl, xo = (x + 1) % 4, (x + 3) % 4, (x + 2) % 4
    yo = 1 - y
    sib, xp, xm, yp = dev(y, x, 1 - c), dev(y, xr, c), dev(y, xl, c), dev(yo, x, c)

    started = []

    barrier = pltpu.get_barrier_semaphore()
    for i in FAR + NEAR[:0:-1]:
        pl.semaphore_signal(barrier, inc=1, device_id=((me + i) % NDP, j), device_id_type=MESH)
    chips = [(y, xr), (y, xl), (y, xo), (yo, x)]
    for yy, xx in chips:
        pl.semaphore_signal(barrier, inc=1, device_id=(me, dev(yy, xx, c)), device_id_type=MESH)
    pl.semaphore_signal(barrier, inc=1, device_id=(me, sib), device_id_type=MESH)

    loads = [
        pltpu.make_async_copy(wg_hbm.at[0], wgu.at[:, 0:HID], w_sem.at[0]),
        pltpu.make_async_copy(wu_hbm.at[0], wgu.at[:, HID : 2 * HID], w_sem.at[1]),
        pltpu.make_async_copy(wd_hbm.at[0], wt.at[2 * HID : 3 * HID, :], w_sem.at[2]),
    ]
    acts = [
        pltpu.make_async_copy(ids_hbm, ids_ref, w_sem.at[5]),
        pltpu.make_async_copy(gates_hbm, gates_ref, w_sem.at[6]),
        pltpu.make_async_copy(tok_hbm, ext.at[0:F, 0:TOK], w_sem.at[3]),
        pltpu.make_async_copy(cot_hbm, ext.at[0:F, TOK : 2 * TOK], w_sem.at[4]),
    ]
    for load in acts + loads:
        load.start()
    acts[0].wait()
    acts[1].wait()

    row = iota((256, TOK), 0)
    ahead = sum(jnp.where(row // 16 == n, o, 0) for n, o in enumerate(OFFSETS))
    expert = (ahead + me) % NDP
    in_first = expert < NDP // 2
    member = jnp.where(in_first, ids_ref[0:1, :], ids_ref[1:2, :]) == expert
    tri = (iota((TOK, TOK), 0) < iota((TOK, TOK), 1)).astype(F32).astype(BF)
    before = jnp.dot(member.astype(F32).astype(BF), tri, preferred_element_type=F32)
    pick = jnp.where(
        jnp.logical_and(member, before == (row % 8).astype(F32)), 1.0, 0.0
    )
    is_x = (row % 16) < 8
    pick_x = jnp.where(is_x, pick, 0.0)
    pick_d = jnp.where(is_x, 0.0, pick)
    pick_out[0] = jnp.where(in_first, pick_x, 0.0).astype(BF)
    pick_out[1] = jnp.where(in_first, 0.0, pick_x).astype(BF)
    pick_out[2] = pick_d.astype(BF)
    gates = gates_ref[...].astype(F32)
    line = iota((512 - F, TOK), 0)
    ext[F:512, 0:TOK] = jnp.where(
        line == 0, gates[0:1, :], jnp.where(line == 1, gates[1:2, :], 0.0)
    ).astype(BF)
    ext[F:512, TOK : 2 * TOK] = jnp.zeros((512 - F, TOK), BF)
    for load in acts[2:]:
        load.wait()
    slots = lax.dot_general(
        jnp.concatenate([pick_x, pick_d], axis=1).astype(BF), ext[...],
        (((1,), (1,)), ((), ())), preferred_element_type=F32,
    ).astype(BF)
    sx[...] = slots.reshape(NDP, 16, 512)
    rx[0] = sx[0]

    r = iota((128, 128), 0)
    k = iota((128, 128), 1)
    perm = jnp.where(k == ((r % 16) // 8) * 64 + (r // 16) * 8 + r % 8, 1.0, 0.0).astype(BF)
    nt = (((1,), (1,)), ((), ()))
    acc[...] = jnp.zeros_like(acc)

    pl.semaphore_wait(barrier, NDP - 1 + len(chips) + 1)

    d_copies = [None]
    for n, o in enumerate(OFFSETS):
        if o:
            copy = pltpu.make_async_remote_copy(
                src_ref=sx.at[n], dst_ref=rx.at[n],
                send_sem=d_send.at[n], recv_sem=d_recv.at[n],
                device_id=((me + o) % NDP, j), device_id_type=MESH,
            )
            copy.start()
            d_copies.append(copy)
            started.append(copy)

    for load in loads:
        load.wait()

    def turn(i, carry):
        at = pl.ds(pl.multiple_of(i * C, 128), C)
        wt[0 : 2 * HID, at] = wgu[at, :].T
        return carry

    lax.fori_loop(0, D // C, turn, 0)

    al = (al0, al1)

    def piece(h, b, lo, n):
        return al[h].at[pl.ds(pl.multiple_of(b * F + lo, 16), n)]

    def move(h, b, lo, n, to, s, sems):
        ref = piece(h, b, lo, n)
        return pltpu.make_async_remote_copy(
            src_ref=ref, dst_ref=ref,
            send_sem=sems[0].at[h, s], recv_sem=sems[1].at[h, s],
            device_id=(me, to), device_id_type=MESH,
        )

    def push(h, b, lo, n, to, s):
        copy = move(h, b, lo, n, to, s, (g_send, g_recv))
        copy.start()
        started.append(copy)

    def share(h, b, lo, n, s):
        copy = move(h, b, lo, n, sib, s, (sib_send, sib_recv))
        copy.start()
        started.append(copy)

    def got(h, b, lo, n, s):
        move(h, b, lo, n, sib, s, (g_send, g_recv)).wait_recv()

    def shared(h, b, lo, n, s):
        move(h, b, lo, n, sib, s, (sib_send, sib_recv)).wait_recv()

    def forward(h, chip):
        at = pl.ds(pl.multiple_of(chip * C, 128), C)
        acc[h] += jnp.dot(wt[:, at], al[h][at, :], preferred_element_type=F32)

    gate_rows = [None, None]

    def own(h):
        for n in range(8 * h, 8 * h + 8):
            if d_copies[n] is not None:
                d_copies[n].wait_recv()
        turned = lax.dot_general(
            rx[8 * h : 8 * h + 8].reshape(128, 512), perm,
            (((0,), (0,)), ((), ())), preferred_element_type=F32,
        )
        al[h][pl.ds(pl.multiple_of(j * F, 16), F), :] = turned[0:F].astype(BF)
        gate_rows[h] = jnp.where(me < NDP // 2, turned[F : F + 1], turned[F + 1 : F + 2])
        push(h, j, FA, FB, xp, 4)
        push(h, j, FA, FB, xm, 5)
        push(h, j, 0, FA, yp, 0)
        push(h, j, 0, FA, xp, 1)
        push(h, j, 0, FA, xm, 2)
        push(h, j, FA, FB, yp, 3)
        share(h, j, 0, FA, 0)
        share(h, j, FA, FB, 1)

    arrivals = {
        "Aoo": ((yo, x), 0, FA, 0, 2, ((0, FA, xp, 6), (0, FA, xm, 7))),
        "Axl": ((y, xl), 0, FA, 1, 5, ((0, HA, xp, 12),)),
        "Axr": ((y, xr), 0, FA, 2, 6, ((HA, HA, xm, 13),)),
        "Boo": ((yo, x), FA, FB, 3, 11, ()),
        "Bxl": ((y, xl), FA, FB, 4, 3, ((FA, HB, xp, 8), (FA, FB, yp, 9))),
        "Bxr": ((y, xr), FA, FB, 5, 4, ((FA + HB, HB, xm, 10), (FA, FB, yp, 11))),
        "Aoxl": ((yo, xl), 0, FA, 6, 9, ((0, HA, xp, 16),)),
        "Aoxr": ((yo, xr), 0, FA, 7, 10, ((HA, HA, xm, 17),)),
        "Bxo1": ((y, xo), FA, HB, 8, 7, ((FA, HB, yp, 14),)),
        "Bxo2": ((y, xo), FA + HB, HB, 10, 8, ((FA + HB, HB, yp, 15),)),
        "Boxl": ((yo, xl), FA, FB, 9, 12, ()),
        "Boxr": ((yo, xr), FA, FB, 11, 13, ()),
        "Axo1": ((y, xo), 0, HA, 12, 14, ()),
        "Axo2": ((y, xo), HA, HA, 13, 15, ()),
        "Boxo1": ((yo, xo), FA, HB, 14, 18, ()),
        "Boxo2": ((yo, xo), FA + HB, HB, 15, 19, ()),
        "Aoxo1": ((yo, xo), 0, HA, 16, 16, ()),
        "Aoxo2": ((yo, xo), HA, HA, 17, 17, ()),
    }
    works = {
        "Wown": ((y, x), ((0, FA, 0), (FA, FB, 1))),
        "Wxl": ((y, xl), ((FA, FB, 3), (0, FA, 5))),
        "Wxr": ((y, xr), ((FA, FB, 4), (0, FA, 6))),
        "Woo": ((yo, x), ((0, FA, 2), (FA, FB, 11))),
        "Woxl": ((yo, xl), ((0, FA, 9), (FA, FB, 12))),
        "Woxr": ((yo, xr), ((0, FA, 10), (FA, FB, 13))),
        "Wxo": ((y, xo), ((FA, HB, 7), (FA + HB, HB, 8), (0, HA, 14), (HA, HA, 15))),
        "Woxo": ((yo, xo), ((0, HA, 16), (HA, HA, 17), (FA, HB, 18), (FA + HB, HB, 19))),
    }

    def arrive(h, name):
        (yy, xx), lo, n, s, to_sib, onward = arrivals[name]
        b = dev(yy, xx, c)
        got(h, b, lo, n, s)
        for first, count, to, sem in onward:
            push(h, b, first, count, to, sem)
        share(h, b, lo, n, to_sib)

    def work(h, name):
        (yy, xx), parts = works[name]
        for lo, n, s in parts:
            shared(h, dev(yy, xx, 1 - c), lo, n, s)
        forward(h, yy * 4 + xx)

    gate_terms = [None, None]

    def units(h):
        pg, pu = acc[h, 0:HID, :], acc[h, HID : 2 * HID, :]
        sig = jax.nn.sigmoid(pg)
        act = pg * sig
        hidden = act * pu
        bk = pltpu.roll(acc[h, 2 * HID : 3 * HID, :], 64, 1)
        ok = iota((HID, 128), 1) < 64
        gate_terms[h] = split_gate(
            jnp.sum(
                jnp.where(ok, bk * hidden.astype(BF).astype(F32), 0.0), axis=0, keepdims=True
            )
        )
        dhid = gate_rows[h] * bk
        dg = jnp.where(ok, dhid * pu * sig * (1.0 + pg * (1.0 - sig)), 0.0)
        du = jnp.where(ok, dhid * act, 0.0)
        lanes = slice(128 * h, 128 * h + 128)
        dd[0:HID, lanes] = dg.astype(BF)
        dd[HID : 2 * HID, lanes] = du.astype(BF)
        dd[2 * HID : 3 * HID, lanes] = pltpu.roll(dg, 64, 1).astype(BF)
        dd[3 * HID : 4 * HID, lanes] = pltpu.roll(du, 64, 1).astype(BF)
        hg[h] = pltpu.roll(jnp.where(ok, hidden * gate_rows[h], 0.0), 64, 1).astype(BF)

    def term(b):
        lo = wgu[pl.ds(pl.multiple_of(b * F, 16), FH), :]
        hi = wgu[pl.ds(pl.multiple_of(b * F + FH, 16), FH), :]
        return jnp.dot(lo, dd[0 : 2 * HID, :], preferred_element_type=F32) + jnp.dot(
            hi, dd[2 * HID : 4 * HID, :], preferred_element_type=F32
        )

    def gate_total(*blocks):
        total = sum(block.astype(F32) for block in blocks)
        return jnp.sum(total, axis=0, keepdims=True)

    columns = (xo, xr, xl, x)
    ts_copies, y_copies, yx_copies, x_copies, xy_copies = {}, {}, {}, {}, {}

    def send(copies, key, src, dst, send_sem, recv_sem, to):
        copy = pltpu.make_async_remote_copy(
            src_ref=src, dst_ref=dst, send_sem=send_sem, recv_sem=recv_sem,
            device_id=(me, to), device_id_type=MESH,
        )
        copy.start()
        copies[key] = copy
        started.append(copy)

    def to_sibling(n):
        tsend[n, 0:FH, :] = term(dev((yo, y)[n % 2], columns[n // 2], 1 - c)).astype(BF)
        tsend[n, FH:RB, 0:128] = gate_terms[0]
        tsend[n, FH:RB, 128:256] = gate_terms[1]
        send(ts_copies, n, tsend.at[n], tsib.at[n], ts_send.at[n], ts_recv.at[n], sib)

    def to_chips(n):
        col, mine = n // 2, n % 2
        both = term(dev((yo, y)[mine], columns[col], c))
        ts_copies[n].wait_recv()
        both = both + tsib[n, 0:FH, :].astype(F32)
        for h in (1, 0):
            lanes = slice(128 * h, 128 * h + 128)
            part = both[:, lanes]
            gate_part = gate_total(gate_terms[h], tsib[n, FH:RB, lanes])
            if mine:
                y_keep[h, col] = part[0:YR]
            else:
                y_send[h, col] = part[0:YR].astype(BF)
            if col == 3:
                x_keep[h, mine, 0 : FH - YR, :] = part[YR:FH]
                x_keep[h, mine, FH - YR :, :] = jnp.where(
                    iota((16, 128), 0) == 0, gate_part, 0.0
                )
            else:
                x_send[h, col, mine, 0 : FH - YR, :] = part[YR:FH].astype(BF)
                x_send[h, col, mine, FH - YR :, :] = split_gate(gate_part)
            if h == 1:
                leave(h, n)

    def leave(h, n):
        col, mine = n // 2, n % 2
        if not mine:
            send(
                y_copies, (h, col), y_send.at[h, col], y_recv.at[h, col],
                ys_sem.at[h, col], yr_sem.at[h, col], yp,
            )
        elif col < 3:
            send(
                x_copies, (h, col), x_send.at[h, col], x_recv.at[h, col],
                xs_sem.at[h, col], xr_sem.at[h, col], dev(y, columns[col], c),
            )

    def then_x(h, col):
        y_copies[h, col].wait_recv()
        yx_send[h, col] = (y_keep[h, col] + y_recv[h, col].astype(F32)).astype(BF)
        send(
            yx_copies, (h, col), yx_send.at[h, col], yx_recv.at[h, col],
            yxs_sem.at[h, col], yxr_sem.at[h, col], dev(y, columns[col], c),
        )

    def x_total(h, mine):
        total = x_keep[h, mine]
        for col in range(3):
            total = total + x_recv[h, col, mine].astype(F32)
        return total

    def then_y(h):
        for col in range(3):
            x_copies[h, col].wait_recv()
        total = x_total(h, 0)
        xy_send[h, 0 : FH - YR, :] = total[0 : FH - YR].astype(BF)
        xy_send[h, FH - YR :, :] = split_gate(gate_total(total[FH - YR :]))
        send(xy_copies, h, xy_send.at[h], xy_recv.at[h], xys_sem.at[h], xyr_sem.at[h], yp)

    b_copies = []

    def give_back(h):
        second = x_total(h, 1)
        y_copies[h, 3].wait_recv()
        first = y_keep[h, 3] + y_recv[h, 3].astype(F32)
        for col in range(3):
            yx_copies[h, col].wait_recv()
            first = first + yx_recv[h, col].astype(F32)
        xy_copies[h].wait_recv()
        second = second + xy_recv[h].astype(F32)
        rpad[0:YR, :] = first.astype(BF)
        rpad[YR:FH, :] = second[0 : FH - YR].astype(BF)
        rpad[FH:RB, :] = split_gate(gate_total(second[FH - YR :]))
        rpad[RB:256, :] = jnp.zeros((256 - RB, 128), BF)
        rows = lax.dot_general(perm, rpad[...], nt, preferred_element_type=F32)
        retb[8 * h : 8 * h + 8] = rows.astype(BF).reshape(8, 16, 256)
        for n in range(8 * h, 8 * h + 8):
            o = OFFSETS[n]
            if o:
                copy = pltpu.make_async_remote_copy(
                    src_ref=retb.at[n], dst_ref=ret.at[n],
                    send_sem=b_send.at[n], recv_sem=b_recv.at[n],
                    device_id=((me + NDP - o) % NDP, j), device_id_type=MESH,
                )
                copy.start()
                b_copies.append(copy)
                started.append(copy)
            else:
                ret[0] = retb[0]

    def grads(i, carry):
        at = pl.ds(pl.multiple_of(i * C, 128), C)
        near, far = al0[at, :], al1[at, :]
        both = lax.dot_general(near, dd[0 : 2 * HID, 0:128], nt, preferred_element_type=F32)
        both += lax.dot_general(far, dd[0 : 2 * HID, 128:256], nt, preferred_element_type=F32)
        gate_out[at, :] = both[:, 0:HID].astype(BF)
        up_out[at, :] = both[:, HID : 2 * HID].astype(BF)
        down = lax.dot_general(hg[0], near, nt, preferred_element_type=F32)
        down += lax.dot_general(hg[1], far, nt, preferred_element_type=F32)
        down_out[:, at] = down.astype(BF)
        return carry

    for name in " ".join(ORDER).split():
        h, name = int(name[0]), name[1:]
        if name == "own":
            own(h)
        elif name in arrivals:
            arrive(h, name)
        elif name in works:
            work(h, name)
        elif name == "U":
            units(h)
        elif name[0] == "T":
            to_sibling(int(name[1:]))
        elif name[0] == "C":
            to_chips(int(name[1:]))
        elif name[0] == "N":
            leave(h, int(name[1:]))
        elif name == "Q2":
            then_y(h)
        elif name[:2] == "P2":
            then_x(h, ("xo", "xr", "xl").index(name[2:]))
        elif name == "B":
            give_back(h)
        elif name[0] == "G":
            lax.fori_loop(int(name[1]), int(name[2]), grads, 0)

    for copy in b_copies:
        copy.wait_recv()
    ret_out[...] = ret[...].reshape(256, 256)
    for copy in started:
        copy.wait_send()


def finish_kernel(ret, pick, gate, up, down, gt_out, gg_out, gate_out, up_out, down_out, sems):
    copies = [
        pltpu.make_async_copy(gate, gate_out.at[0], sems.at[0]),
        pltpu.make_async_copy(up, up_out.at[0], sems.at[1]),
        pltpu.make_async_copy(down, down_out.at[0], sems.at[2]),
    ]
    for copy in copies:
        copy.start()
    tn = (((0,), (0,)), ((), ()))
    rows = ret[...]
    one, two, low = (
        lax.dot_general(rows, pick[n], tn, preferred_element_type=F32) for n in range(3)
    )
    gt_out[0:FH, :] = (one + two)[0:FH].astype(BF)
    gt_out[FH:F, :] = low[0:FH].astype(BF)
    gg_out[0:1, :] = one[FH : FH + 1] + one[FH + 1 : FH + 2]
    gg_out[1:2, :] = two[FH : FH + 1] + two[FH + 1 : FH + 2]
    for copy in copies:
        copy.wait()


def per_device(tokens, cotangent, gates, expert_ids, w_gate, w_up, w_down):
    vmem = pl.BlockSpec(memory_space=pltpu.VMEM)
    hbm = pl.BlockSpec(memory_space=pltpu.HBM)
    dma = pltpu.SemaphoreType.DMA
    operands = (tokens.T, cotangent.T, expert_ids.T, gates.T, w_gate, w_up, w_down)
    results = pl.pallas_call(
        comm_kernel,
        out_shape=[
            pltpu.VMEM((256, 256), BF),
            pltpu.VMEM((3, 256, TOK), BF),
            pltpu.VMEM((D, HID), BF),
            pltpu.VMEM((D, HID), BF),
            pltpu.VMEM((HID, D), BF),
        ],
        in_specs=[hbm] * 7,
        out_specs=[vmem] * 5,
        scratch_shapes=[
            pltpu.VMEM((2, TOK), jnp.int32),
            pltpu.VMEM((2, TOK), BF),
            pltpu.VMEM((D, 2 * HID), BF),
            pltpu.VMEM((3 * HID, D), BF),
            pltpu.VMEM((512, 2 * TOK), BF),
            pltpu.VMEM((NDP, 16, 512), BF),
            pltpu.VMEM((NDP, 16, 512), BF),
            pltpu.VMEM((D, 128), BF),
            pltpu.VMEM((D, 128), BF),
            pltpu.VMEM((2, 3 * HID, 128), F32),
            pltpu.VMEM((4 * HID, 256), BF),
            pltpu.VMEM((2, HID, 128), BF),
            pltpu.VMEM((8, RB, 256), BF),
            pltpu.VMEM((8, RB, 256), BF),
            pltpu.VMEM((2, 4, YR, 128), F32),
            pltpu.VMEM((2, 4, YR, 128), BF),
            pltpu.VMEM((2, 4, YR, 128), BF),
            pltpu.VMEM((2, 3, YR, 128), BF),
            pltpu.VMEM((2, 3, YR, 128), BF),
            pltpu.VMEM((2, 2, RB - YR, 128), F32),
            pltpu.VMEM((2, 3, 2, RB - YR, 128), BF),
            pltpu.VMEM((2, 3, 2, RB - YR, 128), BF),
            pltpu.VMEM((2, RB - YR, 128), BF),
            pltpu.VMEM((2, RB - YR, 128), BF),
            pltpu.VMEM((256, 128), BF),
            pltpu.VMEM((NDP, 16, 256), BF),
            pltpu.VMEM((NDP, 16, 256), BF),
            dma((7,)),
            dma((NDP,)), dma((NDP,)),
            dma((2, 18)), dma((2, 18)), dma((2, 20)), dma((2, 20)),
            dma((8,)), dma((8,)), dma((2, 4)), dma((2, 4)), dma((2, 3)), dma((2, 3)),
            dma((2, 3)), dma((2, 3)), dma((2,)), dma((2,)),
            dma((NDP,)), dma((NDP,)),
        ],
        compiler_params=pltpu.CompilerParams(
            collective_id=0, has_side_effects=True, vmem_limit_bytes=40 * 1024 * 1024
        ),
        name="comm",
    )(*(pltpu.with_memory_space_constraint(a, pltpu.HBM) for a in operands))

    gt, gg, gate, up, down = pl.pallas_call(
        finish_kernel,
        out_shape=[
            jax.ShapeDtypeStruct((F, TOK), BF),
            jax.ShapeDtypeStruct((2, TOK), F32),
            jax.ShapeDtypeStruct((1, D, HID), BF),
            jax.ShapeDtypeStruct((1, D, HID), BF),
            jax.ShapeDtypeStruct((1, HID, D), BF),
        ],
        in_specs=[vmem] * 5,
        out_specs=[vmem, vmem, hbm, hbm, hbm],
        scratch_shapes=[dma((3,))],
        compiler_params=pltpu.CompilerParams(vmem_limit_bytes=16 * 1024 * 1024),
        name="finish",
    )(*(pltpu.with_memory_space_constraint(a, pltpu.VMEM) for a in results))
    return gt.T, gg.T, gate, up, down


def solution(mesh):
    in_specs = (
        P("dp", "expert"),
        P("dp", "expert"),
        P("dp", None),
        P("dp", None),
        P("dp", None, "expert"),
        P("dp", None, "expert"),
        P("dp", "expert", None),
    )
    out_specs = (
        P("dp", "expert"),
        P("dp", None),
        P("dp", None, "expert"),
        P("dp", None, "expert"),
        P("dp", "expert", None),
    )
    return jax.shard_map(
        per_device, mesh=mesh, in_specs=in_specs, out_specs=out_specs, check_vma=False
    )
```

time: 61.4 us -> 59.5 us (0.969)
  Pallas kernels: 60.7 us -> 58.8 us
    pallas_call x1, Pallas kernels: 57.5 us -> 55.6 us  [per_device(): pl.pallas_call(comm_kernel, out_shape=[pltpu.VMEM((256, 256), BF), pltpu....]
where the time goes in v5:
time: 59.5 us; the launch traced here: 59.4 us
  Pallas kernels  58.8 us (99%)
  between operations  0.64 us (1%)
    pallas_call x1, Pallas kernels, per_device(): pl.pallas_call(comm_kernel, out_shape=[pltpu.VMEM((256, 256), BF), pltpu....  55.6 us
    pallas_call x1, Pallas kernels, per_device(): pl.pallas_call(finish_kernel, out_shape=[jax.ShapeDtypeStruct((F, TOK), B...  3.14 us

profile of v5, /device:TPU:1, one launch (start us, length us, event | category | flops | bytes accessed | tf_op | source)
XLA Modules:
  0.0 59.4 jit_solution(1071301297931768033)
XLA Ops:
  0.6 55.6 %comm.1 = (bf16[256,256]{1,0:T(8,128)(2,1)S(1)}, bf16[3,256,128]{2,1,0:T(8,128)(2,1)S(1)}, bf16[7168,128]{1,0:T(8,128)(2,1)S(1)}, bf16[7168,128]{1,0:T(8,128)(2,1)S(1)}, bf16[128,7168]{1,0:T(8,128)(2,1)S(1)}) custom-call(bf16[448,128]{1,0:T(8,128)(2,1)} %bitcast.6, bf16[448,128]{1,0:T(8,128)(2,1)} %bitcast.7, s32[2,128]{1,0:T(2,128)} %bitcast.8, ...), custom_call_target="tpu_custom_call" | custom-call | tf_op jit(solution)/shard_map/comm/pallas_call | solution.py:477
  56.3 3.1 %finish.1 = (bf16[448,128]{1,0:T(8,128)(2,1)}, f32[2,128]{1,0:T(2,128)}, bf16[1,7168,128]{2,1,0:T(8,128)(2,1)}, bf16[1,7168,128]{2,1,0:T(8,128)(2,1)}, bf16[1,128,7168]{2,1,0:T(8,128)(2,1)}) custom-call(bf16[256,256]{1,0:T(8,128)(2,1)S(1)} %get-tuple-element.15.ret, bf16[3,256,128]{2,1,0:T(8,128)(2,1)S(1)} %get-tuple-element.16.pick, ...), custom_call_target="tpu_custom_call" | custom-call | tf_op jit(solution)/shard_map/finish/pallas_call | solution.py:529

commit v6 on v5

--- a/solution.py
+++ b/solution.py
@@ -28,6 +28,7 @@
 FAR = (8, 7, 9, 11, 5, 13, 3, 15)
 OFFSETS = NEAR + FAR
 FH = F // 2
+DR = 4 * HID + 16
 YR = 144
 RB = FH + 16
 
@@ -36,10 +37,10 @@
     "1Bxl 1Bxr 1Aoo 0Woo", "1Axl 1Axr 1Boo 0Boxl", "1Wxl 1Wxr 1Woo 0Bxo1",
     "0Bxo2 0Aoxl 0Aoxr 0Boxr", "0Axo1 0Axo2 1Bxo1 1Bxo2", "1Boxl 0Woxl 0Woxr 1Boxr",
     "0Wxo 1Aoxl 1Aoxr 0Boxo1", "1Axo1 1Axo2 0Boxo2 1Boxo1", "0Aoxo1 0Aoxo2 1Woxl 1Boxo2",
-    "1Woxr 1Wxo 0Woxo 1Aoxo1", "1Aoxo2 0U 1Woxo 1U", "0T0 0T1 0T2 0T3",
-    "0T4 0T5 0T6 0T7", "0C0 0C1 0C2 0C3", "0C4 0C5 0C6 0C7",
-    "0N0 0N1 0N2 0N3", "0N4 0N5 0N6 0N7", "1P2xo 1P2xr 1P2xl 1Q2",
-    "0P2xo 0P2xr 0P2xl 0Q2", "0G02 1B 0B 0G28",
+    "1Woxr 1Wxo 0Woxo 1Aoxo1", "1Aoxo2 0U 1Woxo 1U", "0S 0C0 0C1 0C2",
+    "0C3 0C4 0C5 0C6", "0C7 0N0 0N1 0N2", "0N3 0N4 0N5 0N6",
+    "0N7 1P2xo 1P2xr 1P2xl", "1Q2 0P2xo 0P2xr 0P2xl", "0Q2 0G02 1B 0B",
+    "0G28",
 )
 
 
@@ -58,10 +59,10 @@
     tok_hbm, cot_hbm, ids_hbm, gates_hbm, wg_hbm, wu_hbm, wd_hbm,
     ret_out, pick_out, gate_out, up_out, down_out,
     ids_ref, gates_ref, wgu, wt, ext, sx, rx, al0, al1, acc, dd, hg,
-    tsend, tsib, y_keep, y_send, y_recv, yx_send, yx_recv, x_keep, x_send, x_recv, xy_send, xy_recv,
+    dsib, wsib, y_keep, y_send, y_recv, yx_send, yx_recv, x_keep, x_send, x_recv, xy_send, xy_recv,
     rpad, retb, ret,
     w_sem, d_send, d_recv, g_send, g_recv, sib_send, sib_recv,
-    ts_send, ts_recv, ys_sem, yr_sem, yxs_sem, yxr_sem, xs_sem, xr_sem, xys_sem, xyr_sem,
+    ds_send, ds_recv, ws_send, ws_recv, ys_sem, yr_sem, yxs_sem, yxr_sem, xs_sem, xr_sem, xys_sem, xyr_sem,
     b_send, b_recv,
 ):
     me = lax.axis_index("dp")
@@ -155,6 +156,17 @@
     for load in loads:
         load.wait()
 
+    w_copies = []
+    for q in range(8):
+        copy = pltpu.make_async_remote_copy(
+            src_ref=wgu.at[pl.ds(pl.multiple_of(q * C + (1 - c) * F, 16), F)], dst_ref=wsib.at[q],
+            send_sem=ws_send.at[q], recv_sem=ws_recv.at[q],
+            device_id=(me, sib), device_id_type=MESH,
+        )
+        copy.start()
+        w_copies.append(copy)
+        started.append(copy)
+
     def turn(i, carry):
         at = pl.ds(pl.multiple_of(i * C, 128), C)
         wt[0 : 2 * HID, at] = wgu[at, :].T
@@ -261,7 +273,7 @@
             shared(h, dev(yy, xx, 1 - c), lo, n, s)
         forward(h, yy * 4 + xx)
 
-    gate_terms = [None, None]
+    d_sent = [None, None]
 
     def units(h):
         pg, pu = acc[h, 0:HID, :], acc[h, HID : 2 * HID, :]
@@ -270,11 +282,6 @@
         hidden = act * pu
         bk = pltpu.roll(acc[h, 2 * HID : 3 * HID, :], 64, 1)
         ok = iota((HID, 128), 1) < 64
-        gate_terms[h] = split_gate(
-            jnp.sum(
-                jnp.where(ok, bk * hidden.astype(BF).astype(F32), 0.0), axis=0, keepdims=True
-            )
-        )
         dhid = gate_rows[h] * bk
         dg = jnp.where(ok, dhid * pu * sig * (1.0 + pg * (1.0 - sig)), 0.0)
         du = jnp.where(ok, dhid * act, 0.0)
@@ -283,13 +290,26 @@
         dd[HID : 2 * HID, lanes] = du.astype(BF)
         dd[2 * HID : 3 * HID, lanes] = pltpu.roll(dg, 64, 1).astype(BF)
         dd[3 * HID : 4 * HID, lanes] = pltpu.roll(du, 64, 1).astype(BF)
+        dd[4 * HID : DR, lanes] = split_gate(
+            jnp.sum(
+                jnp.where(ok, bk * hidden.astype(BF).astype(F32), 0.0), axis=0, keepdims=True
+            )
+        )
+        copy = pltpu.make_async_remote_copy(
+            src_ref=dd.at[:, lanes], dst_ref=dsib.at[:, lanes],
+            send_sem=ds_send.at[h], recv_sem=ds_recv.at[h],
+            device_id=(me, sib), device_id_type=MESH,
+        )
+        copy.start()
+        d_sent[h] = copy
+        started.append(copy)
         hg[h] = pltpu.roll(jnp.where(ok, hidden * gate_rows[h], 0.0), 64, 1).astype(BF)
 
-    def term(b):
-        lo = wgu[pl.ds(pl.multiple_of(b * F, 16), FH), :]
-        hi = wgu[pl.ds(pl.multiple_of(b * F + FH, 16), FH), :]
-        return jnp.dot(lo, dd[0 : 2 * HID, :], preferred_element_type=F32) + jnp.dot(
-            hi, dd[2 * HID : 4 * HID, :], preferred_element_type=F32
+    def term(w, first, d):
+        lo = w[pl.ds(first, FH), :]
+        hi = w[pl.ds(first + FH, FH), :]
+        return jnp.dot(lo, d[0 : 2 * HID, :], preferred_element_type=F32) + jnp.dot(
+            hi, d[2 * HID : 4 * HID, :], preferred_element_type=F32
         )
 
     def gate_total(*blocks):
@@ -297,7 +317,7 @@
         return jnp.sum(total, axis=0, keepdims=True)
 
     columns = (xo, xr, xl, x)
-    ts_copies, y_copies, yx_copies, x_copies, xy_copies = {}, {}, {}, {}, {}
+    y_copies, yx_copies, x_copies, xy_copies = {}, {}, {}, {}
 
     def send(copies, key, src, dst, send_sem, recv_sem, to):
         copy = pltpu.make_async_remote_copy(
@@ -308,21 +328,24 @@
         copies[key] = copy
         started.append(copy)
 
-    def to_sibling(n):
-        tsend[n, 0:FH, :] = term(dev((yo, y)[n % 2], columns[n // 2], 1 - c)).astype(BF)
-        tsend[n, FH:RB, 0:128] = gate_terms[0]
-        tsend[n, FH:RB, 128:256] = gate_terms[1]
-        send(ts_copies, n, tsend.at[n], tsib.at[n], ts_send.at[n], ts_recv.at[n], sib)
+    gate_parts = []
+
+    def with_sibling():
+        for copy in w_copies + d_sent:
+            copy.wait_recv()
+        for h in (0, 1):
+            lanes = slice(128 * h, 128 * h + 128)
+            gate_parts.append(gate_total(dd[4 * HID : DR, lanes], dsib[4 * HID : DR, lanes]))
 
     def to_chips(n):
         col, mine = n // 2, n % 2
-        both = term(dev((yo, y)[mine], columns[col], c))
-        ts_copies[n].wait_recv()
-        both = both + tsib[n, 0:FH, :].astype(F32)
+        chip = (yo, y)[mine] * 4 + columns[col]
+        both = term(wgu, pl.multiple_of(chip * C + c * F, 16), dd)
+        both = both + term(wsib.at[chip], 0, dsib)
         for h in (1, 0):
             lanes = slice(128 * h, 128 * h + 128)
             part = both[:, lanes]
-            gate_part = gate_total(gate_terms[h], tsib[n, FH:RB, lanes])
+            gate_part = gate_parts[h]
             if mine:
                 y_keep[h, col] = part[0:YR]
             else:
@@ -426,8 +449,8 @@
             work(h, name)
         elif name == "U":
             units(h)
-        elif name[0] == "T":
-            to_sibling(int(name[1:]))
+        elif name == "S":
+            with_sibling()
         elif name[0] == "C":
             to_chips(int(name[1:]))
         elif name[0] == "N":
@@ -449,11 +472,14 @@
 
 
 def finish_kernel(ret, pick, gate, up, down, gt_out, gg_out, gate_out, up_out, down_out, sems):
-    copies = [
-        pltpu.make_async_copy(gate, gate_out.at[0], sems.at[0]),
-        pltpu.make_async_copy(up, up_out.at[0], sems.at[1]),
-        pltpu.make_async_copy(down, down_out.at[0], sems.at[2]),
-    ]
+    copies = []
+    for n in range(4):
+        rows, units = pl.ds(n * (D // 4), D // 4), pl.ds(n * (HID // 4), HID // 4)
+        copies += [
+            pltpu.make_async_copy(gate.at[rows], gate_out.at[0, rows], sems.at[3 * n]),
+            pltpu.make_async_copy(up.at[rows], up_out.at[0, rows], sems.at[3 * n + 1]),
+            pltpu.make_async_copy(down.at[units], down_out.at[0, units], sems.at[3 * n + 2]),
+        ]
     for copy in copies:
         copy.start()
     tn = (((0,), (0,)), ((), ()))
@@ -496,10 +522,10 @@
             pltpu.VMEM((D, 128), BF),
             pltpu.VMEM((D, 128), BF),
             pltpu.VMEM((2, 3 * HID, 128), F32),
-            pltpu.VMEM((4 * HID, 256), BF),
+            pltpu.VMEM((DR, 256), BF),
             pltpu.VMEM((2, HID, 128), BF),
-            pltpu.VMEM((8, RB, 256), BF),
-            pltpu.VMEM((8, RB, 256), BF),
+            pltpu.VMEM((DR, 256), BF),
+            pltpu.VMEM((8, F, 2 * HID), BF),
             pltpu.VMEM((2, 4, YR, 128), F32),
             pltpu.VMEM((2, 4, YR, 128), BF),
             pltpu.VMEM((2, 4, YR, 128), BF),
@@ -516,7 +542,7 @@
             dma((7,)),
             dma((NDP,)), dma((NDP,)),
             dma((2, 18)), dma((2, 18)), dma((2, 20)), dma((2, 20)),
-            dma((8,)), dma((8,)), dma((2, 4)), dma((2, 4)), dma((2, 3)), dma((2, 3)),
+            dma((2,)), dma((2,)), dma((8,)), dma((8,)), dma((2, 4)), dma((2, 4)), dma((2, 3)), dma((2, 3)),
             dma((2, 3)), dma((2, 3)), dma((2,)), dma((2,)),
             dma((NDP,)), dma((NDP,)),
         ],
@@ -537,7 +563,7 @@
         ],
         in_specs=[vmem] * 5,
         out_specs=[vmem, vmem, hbm, hbm, hbm],
-        scratch_shapes=[dma((3,))],
+        scratch_shapes=[dma((12,))],
         compiler_params=pltpu.CompilerParams(vmem_limit_bytes=16 * 1024 * 1024),
         name="finish",
     )(*(pltpu.with_memory_space_constraint(a, pltpu.VMEM) for a in results))

time: 59.5 us -> 59 us (level); the launches traced: 59.4 us -> 58.2 us
  Pallas kernels: 58.8 us -> 57.5 us
    pallas_call x1, Pallas kernels: 55.6 us -> 54.3 us  [per_device(): pl.pallas_call(comm_kernel, out_shape=[pltpu.VMEM((256, 256), BF), pltpu....]
where the time goes in v6:
time: 59 us; the launch traced here: 58.2 us
  Pallas kernels  57.5 us (97%)
  between operations  0.64 us (1%)
    pallas_call x1, Pallas kernels, per_device(): pl.pallas_call(comm_kernel, out_shape=[pltpu.VMEM((256, 256), BF), pltpu....  54.3 us
    pallas_call x1, Pallas kernels, per_device(): pl.pallas_call(finish_kernel, out_shape=[jax.ShapeDtypeStruct((F, TOK), B...  3.2 us

profile of v6, /device:TPU:1, one launch (start us, length us, event | category | flops | bytes accessed | tf_op | source)
XLA Modules:
  0.0 58.2 jit_solution(5104961530568138358)
XLA Ops:
  0.6 54.3 %comm.1 = (bf16[256,256]{1,0:T(8,128)(2,1)S(1)}, bf16[3,256,128]{2,1,0:T(8,128)(2,1)S(1)}, bf16[7168,128]{1,0:T(8,128)(2,1)S(1)}, bf16[7168,128]{1,0:T(8,128)(2,1)S(1)}, bf16[128,7168]{1,0:T(8,128)(2,1)S(1)}) custom-call(bf16[448,128]{1,0:T(8,128)(2,1)} %bitcast.6, bf16[448,128]{1,0:T(8,128)(2,1)} %bitcast.7, s32[2,128]{1,0:T(2,128)} %bitcast.8, ...), custom_call_target="tpu_custom_call" | custom-call | tf_op jit(solution)/shard_map/comm/pallas_call | solution.py:503
  55.0 3.2 %finish.1 = (bf16[448,128]{1,0:T(8,128)(2,1)}, f32[2,128]{1,0:T(2,128)}, bf16[1,7168,128]{2,1,0:T(8,128)(2,1)}, bf16[1,7168,128]{2,1,0:T(8,128)(2,1)}, bf16[1,128,7168]{2,1,0:T(8,128)(2,1)}) custom-call(bf16[256,256]{1,0:T(8,128)(2,1)S(1)} %get-tuple-element.15.ret, bf16[3,256,128]{2,1,0:T(8,128)(2,1)S(1)} %get-tuple-element.16.pick, ...), custom_call_target="tpu_custom_call" | custom-call | tf_op jit(solution)/shard_map/finish/pallas_call | solution.py:555

commit v7 on v6

--- a/solution.py
+++ b/solution.py
@@ -33,11 +33,11 @@
 RB = FH + 16
 
 ORDER = (
-    "0own 0Wown 1own 0Aoo", "0Bxl 0Bxr 0Axl 0Axr", "0Boo 1Wown 0Wxl 0Wxr",
-    "1Bxl 1Bxr 1Aoo 0Woo", "1Axl 1Axr 1Boo 0Boxl", "1Wxl 1Wxr 1Woo 0Bxo1",
-    "0Bxo2 0Aoxl 0Aoxr 0Boxr", "0Axo1 0Axo2 1Bxo1 1Bxo2", "1Boxl 0Woxl 0Woxr 1Boxr",
-    "0Wxo 1Aoxl 1Aoxr 0Boxo1", "1Axo1 1Axo2 0Boxo2 1Boxo1", "0Aoxo1 0Aoxo2 1Woxl 1Boxo2",
-    "1Woxr 1Wxo 0Woxo 1Aoxo1", "1Aoxo2 0U 1Woxo 1U", "0S 0C0 0C1 0C2",
+    "0own 1own 0Aoo 0Bxl", "0Bxr 0Axl 0Axr 0Boo", "1Bxl 1Bxr 1Aoo 1Axl",
+    "1Axr 0Wown 1Wown 1Boo", "0Wxl 0Wxr 0Woo 0Boxl", "0Bxo1 0Bxo2 0Aoxl 0Aoxr",
+    "0Boxr 0Axo1 0Axo2 1Bxo1", "1Bxo2 1Wxl 1Wxr 1Woo", "1Boxl 1Boxr 1Aoxl 1Aoxr",
+    "0Woxl 0Woxr 0Wxo 0Boxo1", "1Axo1 1Axo2 1Woxl 0Boxo2", "1Boxo1 0Aoxo1 0Aoxo2 1Boxo2",
+    "1Woxr 1Wxo 1Aoxo1 1Aoxo2", "0Woxo 0U 1Woxo 1U", "0S 0C0 0C1 0C2",
     "0C3 0C4 0C5 0C6", "0C7 0N0 0N1 0N2", "0N3 0N4 0N5 0N6",
     "0N7 1P2xo 1P2xr 1P2xl", "1Q2 0P2xo 0P2xr 0P2xl", "0Q2 0G02 1B 0B",
     "0G28",

time: 59 us -> 58.1 us (0.985); the launches traced: 58.2 us -> 58.1 us
  no operation moved by 1% of the time
where the time goes in v7:
time: 58.1 us
  Pallas kernels  57.4 us (99%)
  between operations  0.64 us (1%)
    pallas_call x1, Pallas kernels, per_device(): pl.pallas_call(comm_kernel, out_shape=[pltpu.VMEM((256, 256), BF), pltpu....  54.2 us
    pallas_call x1, Pallas kernels, per_device(): pl.pallas_call(finish_kernel, out_shape=[jax.ShapeDtypeStruct((F, TOK), B...  3.2 us

profile of v7, /device:TPU:1, one launch (start us, length us, event | category | flops | bytes accessed | tf_op | source)
XLA Modules:
  0.0 58.1 jit_solution(14553285679459716809)
XLA Ops:
  0.6 54.2 %comm.1 = (bf16[256,256]{1,0:T(8,128)(2,1)S(1)}, bf16[3,256,128]{2,1,0:T(8,128)(2,1)S(1)}, bf16[7168,128]{1,0:T(8,128)(2,1)S(1)}, bf16[7168,128]{1,0:T(8,128)(2,1)S(1)}, bf16[128,7168]{1,0:T(8,128)(2,1)S(1)}) custom-call(bf16[448,128]{1,0:T(8,128)(2,1)} %bitcast.6, bf16[448,128]{1,0:T(8,128)(2,1)} %bitcast.7, s32[2,128]{1,0:T(2,128)} %bitcast.8, ...), custom_call_target="tpu_custom_call" | custom-call | tf_op jit(solution)/shard_map/comm/pallas_call | solution.py:503
  54.9 3.2 %finish.1 = (bf16[448,128]{1,0:T(8,128)(2,1)}, f32[2,128]{1,0:T(2,128)}, bf16[1,7168,128]{2,1,0:T(8,128)(2,1)}, bf16[1,7168,128]{2,1,0:T(8,128)(2,1)}, bf16[1,128,7168]{2,1,0:T(8,128)(2,1)}) custom-call(bf16[256,256]{1,0:T(8,128)(2,1)S(1)} %get-tuple-element.15.ret, bf16[3,256,128]{2,1,0:T(8,128)(2,1)S(1)} %get-tuple-element.16.pick, ...), custom_call_target="tpu_custom_call" | custom-call | tf_op jit(solution)/shard_map/finish/pallas_call | solution.py:555
